TPU v7x, 32 devices: a whole 2x2x4 slice. The times are simulated.
32 devices in a mesh: row: 4 (over y, x), col: 8 (over z, core).
Axes of the slice: x: 2, y: 2, z: 4, core: 2. Of those that a mesh axis runs over, the one named last changes fastest.
Arguments:
- inputs: bfloat16 [256, 8192], P('col', 'row'), may hold values from -6 to 6
- gate_weight: bfloat16 [8192, 28672], P('row', 'col'), may hold values from -0.0625 to 0.0625
- up_weight: bfloat16 [8192, 28672], P('row', 'col'), may hold values from -0.0625 to 0.0625
- down_weight: bfloat16 [28672, 8192], P('col', 'row'), may hold values from -0.03125 to 0.03125
- out_grad: bfloat16 [256, 8192], P('col', 'row'), may hold values from -1.5 to 1.5
Outputs:
- output: bfloat16 [256, 8192], P('col', 'row')
- in_grad: bfloat16 [256, 8192], P('col', 'row')
- gate_grad: bfloat16 [8192, 28672], P('row', 'col')
- up_grad: bfloat16 [8192, 28672], P('row', 'col')
- down_grad: bfloat16 [28672, 8192], P('col', 'row')
All inputs are finite; a program needn't handle non-finite values.
Results may differ from a plain program's by a relative error of at most 0.005.
Values may be sent and summed in bfloat16 or wider, within the bound.
A program may use at most 192 MiB of HBM per device.

v0:
```python
import jax
import jax.numpy as jnp
from jax import lax
from jax.sharding import PartitionSpec as P


def contract_first(left, right):
    return lax.dot_general(
        left, right, (((0,), (0,)), ((), ())), preferred_element_type=jnp.float32
    )


def contract_last(left, right):
    return lax.dot_general(
        left, right, (((1,), (1,)), ((), ())), preferred_element_type=jnp.float32
    )


def gating(gate_value, up_value):
    sigmoid_gate = jax.nn.sigmoid(gate_value)
    return (gate_value * sigmoid_gate * up_value).astype(jnp.bfloat16)


def gating_grads(hidden_grad, gate_value, up_value):
    sigmoid_gate = jax.nn.sigmoid(gate_value)
    slope = sigmoid_gate * (1.0 + gate_value * (1.0 - sigmoid_gate))
    gate_part = (hidden_grad * up_value * slope).astype(jnp.bfloat16)
    up_part = (hidden_grad * gate_value * sigmoid_gate).astype(jnp.bfloat16)
    return (gate_part, up_part)


def on_device(inputs, gate_weight, up_weight, down_weight, out_grad):
    all_inputs, all_grads = (
        lax.all_gather(inputs, "col", axis=0, tiled=True),
        lax.all_gather(out_grad, "col", axis=0, tiled=True),
    )
    gate_value, up_value = lax.psum(
        (
            jnp.dot(all_inputs, gate_weight, preferred_element_type=jnp.float32),
            jnp.dot(all_inputs, up_weight, preferred_element_type=jnp.float32),
        ),
        "row",
    )
    hidden = gating(gate_value, up_value)
    hidden_grad = lax.psum(contract_last(all_grads, down_weight), "row")
    gate_part, up_part = gating_grads(hidden_grad, gate_value, up_value)
    output = lax.psum_scatter(
        jnp.dot(hidden, down_weight, preferred_element_type=jnp.float32),
        "col",
        scatter_dimension=0,
        tiled=True,
    ).astype(jnp.bfloat16)
    in_grad = lax.psum_scatter(
        contract_last(gate_part, gate_weight) + contract_last(up_part, up_weight),
        "col",
        scatter_dimension=0,
        tiled=True,
    ).astype(jnp.bfloat16)
    gate_grad = contract_first(all_inputs, gate_part).astype(jnp.bfloat16)
    up_grad = contract_first(all_inputs, up_part).astype(jnp.bfloat16)
    down_grad = contract_first(hidden, all_grads).astype(jnp.bfloat16)
    return (output, in_grad, gate_grad, up_grad, down_grad)


def solution(mesh):
    in_specs = (P("col", "row"), P("row", "col"), P("row", "col"), P("col", "row"), P("col", "row"))
    out_specs = (
        P("col", "row"),
        P("col", "row"),
        P("row", "col"),
        P("row", "col"),
        P("col", "row"),
    )
    return jax.shard_map(
        on_device, mesh=mesh, in_specs=in_specs, out_specs=out_specs, check_vma=False
    )
```

profile of v0, /device:TPU:0, one launch (start us, length us, event | category | flops | bytes accessed | tf_op | source)
XLA Modules:
  0.0 393.8 jit_solution(201801335477085230)
XLA Ops:
  7.2 0.0 all-gather.3.cloned.1.call-start
  7.2 0.7 all-gather.3.cloned.1.call-update
  7.9 0.0 all-gather.5.cloned.1.call-start
  7.9 0.7 all-gather.5.cloned.1.call-update
  8.6 0.0 all-reduce.3.cloned.1.call-start
  8.7 25.7 %all-gather.3.cloned.1.call-done = bf16[256,2048]{1,0:T(8,128)(2,1)} async-done(((bf16[32,2048]{1,0:T(8,128)(2,1)}), bf16[256,2048]{1,0:T(8,128)(2,1)}) %all-gather.3.cloned.1.call-update) | async-done | bytes 1048592 | tf_op jit(solution)/shard_map/all_gather | solution.py:34
  34.4 0.0 copy-start.1
  34.4 11.4 %fusion.3 = f32[256,3584]{1,0:T(8,128)} fusion(bf16[256,2048]{1,0:T(8,128)(2,1)} %all-gather.3.cloned.1.call-done, bf16[2048,3584]{1,0:T(8,128)(2,1)} %param.7), kind=kOutput, calls=%fused_computation.11 | convolution fusion | flops 3758096384 | bytes 19398656 | tf_op jit(solution)/shard_map/dot_general | solution.py:40
  45.8 0.0 copy-done.1
  45.8 9.2 %fusion.2 = f32[256,3584]{1,0:T(8,128)} fusion(bf16[256,2048]{1,0:T(8,128)(2,1)S(1)} %copy-done.1, bf16[2048,3584]{1,0:T(8,128)(2,1)} %param.6), kind=kOutput, calls=%fused_computation.10 | convolution fusion | flops 3758096384 | bytes 19398656 | tf_op jit(solution)/shard_map/dot_general | solution.py:39
  55.0 2.9 all-gather.5.cloned.1.call-done
  57.8 11.3 %fusion.5 = f32[256,3584]{1,0:T(8,128)} fusion(bf16[256,2048]{1,0:T(8,128)(2,1)} %all-gather.5.cloned.1.call-done, bf16[3584,2048]{1,0:T(8,128)(2,1)} %param.8), kind=kOutput, calls=%fused_computation.13 | convolution fusion | flops 3758096384 | bytes 19398656 | tf_op jit(solution)/shard_map/dot_general | solution.py:14
  69.2 0.0 all-reduce.3.cloned.1.call-update
  69.2 0.0 reduce-scatter.3.cloned.1.call-start
  69.2 215.1 %all-reduce.3.cloned.1.call-done = (f32[256,3584]{1,0:T(8,128)}, f32[256,3584]{1,0:T(8,128)}, f32[256,3584]{1,0:T(8,128)}) async-done(((f32[256,3584]{1,0:T(8,128)}, f32[256,3584]{1,0:T(8,128)}, f32[256,3584]{1,0:T(8,128)}), (f32[256,3584]{1,0:T(8,128)}, f32[256,3584]{1,0:T(8,128)}, f32[256,3584]{1,0:T(8,128)})) %all-reduce.3.cloned.1.call-update) | async-done | bytes 11010064 | tf_op jit(solution)/shard_map/psum | solution.py:37
  284.3 6.6 %multiply_convert_fusion = (bf16[256,3584]{1,0:T(8,128)(2,1)}, bf16[256,3584]{1,0:T(8,128)(2,1)}, bf16[256,3584]{1,0:T(8,128)(2,1)S(1)}) fusion(f32[256,3584]{1,0:T(8,128)} %get-tuple-element.12, f32[256,3584]{1,0:T(8,128)} %get-tuple-element.11, f32[256,3584]{1,0:T(8,128)} %get-tuple-element.10), kind=kLoop, calls=%fused_computation.5 | loop fusion | flops 14680064 | bytes 16515072 | tf_op jit(solution)/shard_map/convert_element_type | solution.py:28
  290.9 8.7 %fusion.4 = f32[256,2048]{1,0:T(8,128)} fusion(bf16[256,3584]{1,0:T(8,128)(2,1)S(1)} %get-tuple-element.15, bf16[3584,2048]{1,0:T(8,128)(2,1)} %param.8), kind=kOutput, calls=%fused_computation.12 | convolution fusion | flops 3758096384 | bytes 18612224 | tf_op jit(solution)/shard_map/dot_general | solution.py:48
  299.6 0.0 reduce-scatter.3.cloned.1.call-update
  299.6 0.2 reduce-scatter.5.cloned.1.call-start
  299.9 0.0 copy-start
  299.9 11.2 %fusion.6 = f32[256,2048]{1,0:T(8,128)} fusion(bf16[256,3584]{1,0:T(8,128)(2,1)} %get-tuple-element.14, bf16[2048,3584]{1,0:T(8,128)(2,1)} %param.6), kind=kOutput, calls=%fused_computation.14 | convolution fusion | flops 3758096384 | bytes 18612224 | tf_op jit(solution)/shard_map/dot_general | solution.py:14
  311.0 0.0 copy-done
  311.0 9.7 %convolution_add_fusion = f32[256,2048]{1,0:T(8,128)} fusion(f32[256,2048]{1,0:T(8,128)} %fusion.6, bf16[256,3584]{1,0:T(8,128)(2,1)S(1)} %copy-done, bf16[2048,3584]{1,0:T(8,128)(2,1)} %param.7), kind=kOutput, calls=%fused_computation.9 | convolution fusion | flops 3758620672 | bytes 20709376 | tf_op jit(solution)/shard_map/dot_general | solution.py:14
  320.7 0.0 reduce-scatter.5.cloned.1.call-update
  320.8 9.1 %fusion = bf16[2048,3584]{0,1:T(8,128)(2,1)} fusion(bf16[256,3584]{1,0:T(8,128)(2,1)} %get-tuple-element.14, bf16[256,2048]{1,0:T(8,128)(2,1)S(1)} %copy-done.1), kind=kOutput, calls=%fused_computation.3 | convolution fusion | flops 3765436416 | bytes 17563648 | tf_op jit(solution)/shard_map/dot_general | solution.py:8
  329.9 18.7 %copy.10 = bf16[2048,3584]{1,0:T(8,128)(2,1)} copy(bf16[2048,3584]{0,1:T(8,128)(2,1)} %fusion) | data formatting | bytes 29360128
  348.6 9.1 %fusion.1 = bf16[2048,3584]{0,1:T(8,128)(2,1)} fusion(bf16[256,3584]{1,0:T(8,128)(2,1)} %get-tuple-element.13, bf16[256,2048]{1,0:T(8,128)(2,1)S(1)} %copy-done.1), kind=kOutput, calls=%fused_computation.4 | convolution fusion | flops 3765436416 | bytes 17563648 | tf_op jit(solution)/shard_map/dot_general | solution.py:8
  357.6 18.8 %copy.11 = bf16[2048,3584]{1,0:T(8,128)(2,1)} copy(bf16[2048,3584]{0,1:T(8,128)(2,1)} %fusion.1) | data formatting | bytes 29360128
  376.4 0.0 copy-done.2
  376.4 7.6 %convolution_convert_fusion = bf16[3584,2048]{1,0:T(8,128)(2,1)} fusion(bf16[256,3584]{1,0:T(8,128)(2,1)S(1)} %get-tuple-element.15, bf16[256,2048]{1,0:T(8,128)(2,1)S(1)} %copy-done.2), kind=kOutput, calls=%fused_computation | convolution fusion | flops 3765436416 | bytes 17563648 | tf_op jit(solution)/shard_map/dot_general | solution.py:8
  384.0 1.6 convert_element_type.31
  385.6 1.6 convert_element_type.34
  (3 shorter events, 0.0 us)
Async XLA Ops:
  7.2 27.3 %all-gather.3.cloned.1.call-start = ((), (), s32[]{:S(2)}) async-start(), calls=%async_computation.2 | async-start | bytes 1179648 | tf_op jit(solution)/shard_map/all_gather | solution.py:34
  7.9 49.9 %all-gather.5.cloned.1.call-start = ((), (), s32[]{:S(2)}) async-start(), calls=%async_computation.4 | async-start | bytes 1179648 | tf_op jit(solution)/shard_map/all_gather | solution.py:35
  8.6 275.7 %all-reduce.3.cloned.1.call-start = ((), (), s32[]{:S(2)}) async-start(), calls=%async_computation.6 | async-start | bytes 22020096 | tf_op jit(solution)/shard_map/psum | solution.py:37
  34.4 11.4 %copy-start.1 = (bf16[256,2048]{1,0:T(8,128)(2,1)S(1)}, bf16[256,2048]{1,0:T(8,128)(2,1)}, u32[]{:S(2)}) copy-start(bf16[256,2048]{1,0:T(8,128)(2,1)} %all-gather.3.cloned.1.call-done) | copy-start | bytes 3145732
  69.2 314.8 %reduce-scatter.3.cloned.1.call-start = ((), (), s32[]{:S(2)}) async-start(), calls=%async_computation.3 | async-start | bytes 2359296 | tf_op jit(solution)/shard_map/reduce_scatter | solution.py:47
  299.6 86.0 %reduce-scatter.5.cloned.1.call-start = ((), (), s32[]{:S(2)}) async-start(), calls=%async_computation.5 | async-start | bytes 2359296 | tf_op jit(solution)/shard_map/reduce_scatter | solution.py:53
  299.9 11.2 %copy-start = (bf16[256,3584]{1,0:T(8,128)(2,1)S(1)}, bf16[256,3584]{1,0:T(8,128)(2,1)}, u32[]{:S(2)}) copy-start(bf16[256,3584]{1,0:T(8,128)(2,1)} %get-tuple-element.13) | copy-start | bytes 5505028
  357.6 18.8 %copy-start.2 = (bf16[256,2048]{1,0:T(8,128)(2,1)S(1)}, bf16[256,2048]{1,0:T(8,128)(2,1)}, u32[]{:S(2)}) copy-start(bf16[256,2048]{1,0:T(8,128)(2,1)} %all-gather.5.cloned.1.call-done) | copy-start | bytes 3145732
Sparse Core Ops, SparseCore 0:
  9.6 24.7 all-gather.2
  36.0 21.7 all-gather.4
  69.3 214.9 all-reduce.2
  299.7 35.7 reduce-scatter.2
  337.7 34.3 reduce-scatter.4
where the time goes:
time: 395 us; the launch traced here: 394 us
  waiting for transfers between devices  245 us (62%)
  matrix products  87.2 us (22%)
  local copies, waits for them, and re-layouts  37.5 us (9%)
  between operations  13.8 us (3%)
  other arithmetic  9.8 us (2%)
    psum x1, waiting for transfers between devices, on_device(): lax.psum((jnp.dot(all_inputs, gate_weight, preferred_element_type=jnp.flo...  215 us
    unnamed x8, local copies, waits for them, and re-layouts  37.5 us
    dot_general x3, matrix products, contract_last(): lax.dot_general(left, right, (((1,), (1,)), ((), ())), preferred_element_...  32.2 us
    dot_general x3, matrix products, contract_first(): lax.dot_general(left, right, (((0,), (0,)), ((), ())), preferred_element_...  25.8 us
    all_gather x1, waiting for transfers between devices, on_device(): lax.all_gather(inputs, 'col', axis=0, tiled=True)  25.7 us
    dot_general x1, matrix products, on_device(): jnp.dot(all_inputs, up_weight, preferred_element_type=jnp.float32)  11.4 us
    dot_general x1, matrix products, on_device(): jnp.dot(all_inputs, gate_weight, preferred_element_type=jnp.float32)  9.16 us
    dot_general x1, matrix products, on_device(): jnp.dot(hidden, down_weight, preferred_element_type=jnp.float32)  8.74 us
  transfers between devices with their start and end apart: 5, of which 3 were waited for; matrix products, arithmetic and copies ran while one was open for 27% of the time, Pallas kernels for 0%

commit v1 on v0

v1 whole, which is shorter than its diff:
```python
import functools
import math

import jax
import jax.numpy as jnp
from jax import lax
from jax.experimental import pallas as pl
from jax.experimental.pallas import tpu as pltpu
from jax.sharding import PartitionSpec as P

MESH = pl.DeviceIdType.MESH
RING = 4
LAG = 2


def contract_first(left, right):
    return lax.dot_general(
        left, right, (((0,), (0,)), ((), ())), preferred_element_type=jnp.float32
    )


def contract_last(left, right):
    return lax.dot_general(
        left, right, (((1,), (1,)), ((), ())), preferred_element_type=jnp.float32
    )


def units_of(hidden_block):
    for units in (14, 28, 2):
        if hidden_block % (units * 128) == 0:
            return units
    return 2


def mix_kernel(
    side, planes, units,
    x_ref, og_ref, wg_ref, wu_ref, wd_ref,
    x_out, og_out, h_out, gp_out, up_out, acc_out, acc_in,
    xf, of, wgu, wdn, p_gu, p_h, own_gu, own_h, r1_gu, r1_h, p2_gu, p2_h, r2_gu, r2_h,
    full, stage, tmp,
    gz_send, gz_recv, gs_send, gs_recv,
    rs_send, rs_recv, ld_gu, ld_d, io_sem, st_sem,
):
    n, unit = side, wgu.shape[-1]
    owners = n * n
    tokens, width = xf.shape
    token_block = tokens // owners
    share = tokens // (2 * planes)
    pairs = units // 2
    row, col = lax.axis_index("row"), lax.axis_index("col")
    my_y, my_x = row // n, row % n
    z, core = col // 2, col % 2
    sibling = (row, z * 2 + (1 - core))

    def along_x(m):
        return (my_y * n + m, col)

    def along_y(m):
        return (m * n + my_x, col)

    firsts = ((my_x, along_x, my_y, along_y), (my_y, along_y, my_x, along_x))

    def slot_of(par, owner):
        oy, ox = owner // n, owner % n
        return ox * n + oy if par == 0 else oy * n + ox

    def plane(d):
        return (z + d) % planes

    partners = [sibling]
    for d in range(1, planes):
        partners.append((row, plane(d) * 2 + core))
    for d in range(1, n):
        partners.append(along_x((my_x + d) % n))
        partners.append(along_y((my_y + d) % n))
    barrier = pltpu.get_barrier_semaphore()
    for partner in partners:
        pl.semaphore_signal(barrier, inc=1, device_id=partner, device_id_type=MESH)

    def columns(k):
        return pl.ds(pl.multiple_of((k % units) * unit, 128), unit)

    def load_gu(k):
        s = k % RING
        return [
            pltpu.make_async_copy(ref.at[:, columns(k)], wgu.at[s, a], ld_gu.at[s, a])
            for a, ref in enumerate((wg_ref, wu_ref))
        ]

    def load_d(k):
        s = k % RING
        return [pltpu.make_async_copy(wd_ref.at[columns(k), :], wdn.at[s], ld_d.at[s])]

    def start(copies):
        for copy in copies:
            copy.start()

    def wait(copies):
        for copy in copies:
            copy.wait()

    for k in range(RING):
        start(load_gu(k))
        start(load_d(k))

    def rows(c):
        return pl.ds(pl.multiple_of(c * share, 16), share)

    def gather_z(a, src, dst, d):
        return pltpu.make_async_remote_copy(
            src_ref=src, dst_ref=dst.at[rows(col)],
            send_sem=gz_send.at[a, d - 1], recv_sem=gz_recv.at[a, d - 1],
            device_id=(row, plane(d) * 2 + core), device_id_type=MESH,
        )

    def gather_s(a, src, dst, d):
        c = ((z + planes - d) % planes) * 2 + core
        return pltpu.make_async_remote_copy(
            src_ref=src if d == 0 else dst.at[rows(c)], dst_ref=dst.at[rows(c)],
            send_sem=gs_send.at[a, d], recv_sem=gs_recv.at[a, d],
            device_id=sibling, device_id_type=MESH,
        )

    def gather_start(a, src, dst):
        for d in range(1, planes):
            gather_z(a, src, dst, d).start()
        gather_s(a, src, dst, 0).start()
        dst[rows(col), :] = src[...]

    def gather_end(a, src, dst):
        for d in range(1, planes):
            gather_z(a, src, dst, d).wait_recv()
            gather_s(a, src, dst, d).start()
        for d in range(planes):
            gather_s(a, src, dst, d).wait_recv()

    def gather_drain(a, src, dst):
        for d in range(1, planes):
            gather_z(a, src, dst, d).wait_send()
        for d in range(planes):
            gather_s(a, src, dst, d).wait_send()

    def first_send(kind, par, i, d):
        mine, line, _, _ = firsts[par]
        to = (mine + d) % n
        src, dst = ((p_gu, r1_gu), (p_h, r1_h))[kind]
        return pltpu.make_async_remote_copy(
            src_ref=src.at[i, pl.ds(to * n, n)], dst_ref=dst.at[i, d - 1],
            send_sem=rs_send.at[2 * kind, i, d - 1], recv_sem=rs_recv.at[2 * kind, i, d - 1],
            device_id=line(to), device_id_type=MESH,
        )

    def second_send(kind, par, i, d):
        _, _, mine, line = firsts[par]
        src, dst = ((p2_gu, r2_gu), (p2_h, r2_h))[kind]
        return pltpu.make_async_remote_copy(
            src_ref=src.at[i, d - 1], dst_ref=dst.at[i, d - 1],
            send_sem=rs_send.at[2 * kind + 1, i, d - 1],
            recv_sem=rs_recv.at[2 * kind + 1, i, d - 1],
            device_id=line((mine + d) % n), device_id_type=MESH,
        )

    def spread_first(par, i, d):
        mine_f, _, mine_s, line = firsts[par]
        block = full.at[i, mine_f * n + mine_s]
        return pltpu.make_async_remote_copy(
            src_ref=block, dst_ref=block,
            send_sem=rs_send.at[4, i, d - 1], recv_sem=rs_recv.at[4, i, d - 1],
            device_id=line((mine_s + d) % n), device_id_type=MESH,
        )

    def spread_second(par, i, d):
        mine, line, _, _ = firsts[par]
        blocks = full.at[i, pl.ds(mine * n, n)]
        return pltpu.make_async_remote_copy(
            src_ref=blocks, dst_ref=blocks,
            send_sem=rs_send.at[5, i, d - 1], recv_sem=rs_recv.at[5, i, d - 1],
            device_id=line((mine + d) % n), device_id_type=MESH,
        )

    def put_partial(par, i, a, value, partial, own, arrays):
        mine = firsts[par][0]
        for owner in range(owners):
            block = value[owner * token_block:(owner + 1) * token_block]
            tmp[a, slot_of(par, owner)] = block
            partial[i, slot_of(par, owner), a] = block.astype(jnp.bfloat16)
        for s in range(n):
            own[i, s, a] = tmp[a, mine * n + s]

    def project(par, i):
        s = i % RING
        wait(load_gu(i))
        for a in range(2):
            value = jnp.dot(xf[...], wgu[s, a], preferred_element_type=jnp.float32)
            put_partial(par, i, a, value, p_gu, own_gu, 2)
        start(load_gu(i + RING))
        for d in range(1, n):
            first_send(0, par, i, d).start()

    def project_grad(par, i):
        s = i % RING
        wait(load_d(i))
        value = contract_last(of[...], wdn[s])
        put_partial(par, i, 0, value, p_h, own_h, 1)
        start(load_d(i + RING))
        for d in range(1, n):
            first_send(1, par, i, d).start()

    def halfway(kind, par, i):
        mine = firsts[par][2]
        own, got, out = ((own_gu, r1_gu, p2_gu), (own_h, r1_h, p2_h))[kind]
        for d in range(1, n):
            first_send(kind, par, i, d).wait_recv()
        for d in range(1, n):
            s = (mine + d) % n
            for a in range(2 - kind):
                total = own[i, s, a]
                for e in range(n - 1):
                    total = total + got[i, e, s, a].astype(jnp.float32)
                out[i, d - 1, a] = total.astype(jnp.bfloat16)
            second_send(kind, par, i, d).start()

    def total_of(kind, par, i, a):
        mine = firsts[par][2]
        own, got, last = ((own_gu, r1_gu, r2_gu), (own_h, r1_h, r2_h))[kind]
        total = own[i, mine, a]
        for e in range(n - 1):
            total = total + got[i, e, mine, a].astype(jnp.float32)
        for e in range(n - 1):
            total = total + last[i, e, a].astype(jnp.float32)
        return total

    def gate(par, i):
        for kind in range(2):
            for d in range(1, n):
                second_send(kind, par, i, d).wait_recv()
        gate_value = total_of(0, par, i, 0)
        up_value = total_of(0, par, i, 1)
        hidden_grad = total_of(1, par, i, 0)
        sig = jax.nn.sigmoid(gate_value)
        mine = firsts[par][0] * n + firsts[par][2]
        full[i, mine, 0] = (gate_value * sig * up_value).astype(jnp.bfloat16)
        slope = sig * (1.0 + gate_value * (1.0 - sig))
        full[i, mine, 1] = (hidden_grad * up_value * slope).astype(jnp.bfloat16)
        full[i, mine, 2] = (hidden_grad * gate_value * sig).astype(jnp.bfloat16)
        for d in range(1, n):
            spread_first(par, i, d).start()

    def forward(par, i):
        for d in range(1, n):
            spread_first(par, i, d).wait_recv()
        for d in range(1, n):
            spread_second(par, i, d).start()

    def store(i):
        return [
            pltpu.make_async_copy(
                stage.at[a, :, columns(i)], out.at[:, columns(i)], st_sem.at[a, i]
            )
            for a, out in enumerate((h_out, gp_out, up_out))
        ]

    tile = min(512, width)

    def finish(par, i):
        k = units + i
        s = k % RING
        for d in range(1, n):
            spread_second(par, i, d).wait_recv()
        for a in range(3):
            for owner in range(owners):
                stage[a, pl.ds(owner * token_block, token_block), columns(i)] = full[
                    i, slot_of(par, owner), a
                ]
        start(store(i))
        wait(load_gu(k))
        wait(load_d(k))

        def add(t, carry):
            cols = pl.ds(pl.multiple_of(t * tile, 128), tile)
            acc_out[:, cols] += jnp.dot(
                stage[0, :, columns(i)], wdn[s, :, cols], preferred_element_type=jnp.float32
            )
            acc_in[:, cols] += contract_last(
                stage[1, :, columns(i)], wgu[s, 0, cols, :]
            ) + contract_last(stage[2, :, columns(i)], wgu[s, 1, cols, :])
            return carry

        lax.fori_loop(0, width // tile, add, 0)

        @pl.when(k + RING < 2 * units)
        def _():
            start(load_gu(k + RING))
            start(load_d(k + RING))

    pl.semaphore_wait(barrier, len(partners))
    gather_start(0, x_ref, xf)
    acc_out[...] = jnp.zeros_like(acc_out)
    acc_in[...] = jnp.zeros_like(acc_in)
    gather_end(0, x_ref, xf)
    gather_start(1, og_ref, of)

    starts = {}
    starts["project"] = 0
    starts["halfway0"] = LAG
    starts["grad"] = pairs
    starts["halfway1"] = pairs + LAG
    starts["gate"] = pairs + 2 * LAG
    starts["forward"] = pairs + 3 * LAG
    starts["finish"] = pairs + 4 * LAG
    steps = pairs + 4 * LAG + pairs

    def step(t, carry):
        def during(name, work):
            first = starts[name]

            @pl.when(jnp.logical_and(t >= first, t < first + pairs))
            def _():
                for par in range(2):
                    work(par, 2 * (t - first) + par)

        @pl.when(t == pairs)
        def _():
            gather_end(1, og_ref, of)

        during("project", project)
        during("grad", project_grad)
        during("halfway0", functools.partial(halfway, 0))
        during("halfway1", functools.partial(halfway, 1))
        during("gate", gate)
        during("forward", forward)
        during("finish", finish)
        return carry

    lax.fori_loop(0, steps, step, 0)

    outs = [
        pltpu.make_async_copy(xf, x_out, io_sem.at[0]),
        pltpu.make_async_copy(of, og_out, io_sem.at[1]),
    ]
    start(outs)

    def drain(p, carry):
        for par in range(2):
            i = 2 * p + par
            for d in range(1, n):
                for kind in range(2):
                    first_send(kind, par, i, d).wait_send()
                    second_send(kind, par, i, d).wait_send()
                spread_first(par, i, d).wait_send()
                spread_second(par, i, d).wait_send()
            wait(store(i))
        return carry

    lax.fori_loop(0, pairs, drain, 0)
    gather_drain(0, x_ref, xf)
    gather_drain(1, og_ref, of)
    wait(outs)


def mix(mesh, inputs, gate_weight, up_weight, down_weight, out_grad):
    rows, cols = mesh.shape["row"], mesh.shape["col"]
    n = math.isqrt(rows)
    assert n * n == rows and cols % 2 == 0
    planes = cols // 2
    tokens, width = inputs.shape[0] * cols, inputs.shape[1]
    hidden = gate_weight.shape[1]
    units = units_of(hidden)
    u = hidden // units
    tb = tokens // rows
    bf, f32 = jnp.bfloat16, jnp.float32
    dma = pltpu.SemaphoreType.DMA
    vmem = pl.BlockSpec(memory_space=pltpu.VMEM)
    hbm = pl.BlockSpec(memory_space=pl.ANY)
    flops = 12 * tokens * width * hidden
    return pl.pallas_call(
        functools.partial(mix_kernel, n, planes, units),
        out_shape=(
            jax.ShapeDtypeStruct((tokens, width), bf),
            jax.ShapeDtypeStruct((tokens, width), bf),
            jax.ShapeDtypeStruct((tokens, hidden), bf),
            jax.ShapeDtypeStruct((tokens, hidden), bf),
            jax.ShapeDtypeStruct((tokens, hidden), bf),
            jax.ShapeDtypeStruct((tokens, width), f32),
            jax.ShapeDtypeStruct((tokens, width), f32),
        ),
        in_specs=[vmem, vmem, hbm, hbm, hbm],
        out_specs=(hbm, hbm, hbm, hbm, hbm, vmem, vmem),
        scratch_shapes=[
            pltpu.VMEM((tokens, width), bf),
            pltpu.VMEM((tokens, width), bf),
            pltpu.VMEM((RING, 2, width, u), bf),
            pltpu.VMEM((RING, u, width), bf),
            pltpu.VMEM((units, rows, 2, tb, u), bf),
            pltpu.VMEM((units, rows, 1, tb, u), bf),
            pltpu.VMEM((units, n, 2, tb, u), f32),
            pltpu.VMEM((units, n, 1, tb, u), f32),
            pltpu.VMEM((units, n - 1, n, 2, tb, u), bf),
            pltpu.VMEM((units, n - 1, n, 1, tb, u), bf),
            pltpu.VMEM((units, n - 1, 2, tb, u), bf),
            pltpu.VMEM((units, n - 1, 1, tb, u), bf),
            pltpu.VMEM((units, n - 1, 2, tb, u), bf),
            pltpu.VMEM((units, n - 1, 1, tb, u), bf),
            pltpu.VMEM((units, rows, 3, tb, u), bf),
            pltpu.VMEM((3, tokens, hidden), bf),
            pltpu.VMEM((2, rows, tb, u), f32),
            dma((2, planes - 1)),
            dma((2, planes - 1)),
            dma((2, planes)),
            dma((2, planes)),
            dma((6, units, n - 1)),
            dma((6, units, n - 1)),
            dma((RING, 2)),
            dma((RING,)),
            dma((2,)),
            dma((3, units)),
        ],
        compiler_params=pltpu.CompilerParams(
            collective_id=0, has_side_effects=True, vmem_limit_bytes=60 * 2**20
        ),
        cost_estimate=pl.CostEstimate(
            flops=flops, bytes_accessed=12 * width * hidden, transcendentals=0
        ),
    )(inputs, out_grad, gate_weight, up_weight, down_weight)


def on_device(mesh, inputs, gate_weight, up_weight, down_weight, out_grad):
    all_inputs, all_grads, hidden, gate_part, up_part, out_sum, in_sum = mix(
        mesh, inputs, gate_weight, up_weight, down_weight, out_grad
    )
    scatter = functools.partial(
        lax.psum_scatter, axis_name="col", scatter_dimension=0, tiled=True
    )
    output = scatter(out_sum).astype(jnp.bfloat16)
    in_grad = scatter(in_sum).astype(jnp.bfloat16)
    gate_grad = contract_first(all_inputs, gate_part).astype(jnp.bfloat16)
    up_grad = contract_first(all_inputs, up_part).astype(jnp.bfloat16)
    down_grad = contract_first(hidden, all_grads).astype(jnp.bfloat16)
    return (output, in_grad, gate_grad, up_grad, down_grad)


def solution(mesh):
    in_specs = (P("col", "row"), P("row", "col"), P("row", "col"), P("col", "row"), P("col", "row"))
    out_specs = (
        P("col", "row"),
        P("col", "row"),
        P("row", "col"),
        P("row", "col"),
        P("col", "row"),
    )
    return jax.shard_map(
        functools.partial(on_device, mesh),
        mesh=mesh, in_specs=in_specs, out_specs=out_specs, check_vma=False,
    )
```

time: 395 us -> 207 us (0.52)
  waiting for transfers between devices: 245 us -> 48.4 us
  Pallas kernels: 0 us -> 117 us
  matrix products: 87.2 us -> 22.8 us
  local copies, waits for them, and re-layouts: 37.5 us -> 1.05 us
  other arithmetic: 9.8 us -> 3.24 us
    psum x1 -> x0, waiting for transfers between devices: 215 us -> none  [on_device(): lax.psum((jnp.dot(all_inputs, gate_weight, preferred_element_type=jnp.flo...]
    pallas_call x0 -> x1, Pallas kernels: none -> 117 us  [mix(): pl.pallas_call(functools.partial(mix_kernel, n, planes, units), out_shape...]
    dot_general x6 -> x0, matrix products: 61.5 us -> none  [the longest x3 32.2 us: contract_last(): lax.dot_general(left, right, (((1,), (1,)), ((), ())), preferred_element_...]
    reduce_scatter x2, waiting for transfers between devices: 0.01 us -> 47.7 us  [the longest x1 35.1 us: on_device(): in_grad = scatter(in_sum).astype(jnp.bfloat16)]
    unnamed x8 -> x10, local copies, waits for them, and re-layouts: 37.5 us -> 1.05 us
    all_gather x2 -> x0, waiting for transfers between devices: 28.6 us -> none  [the longest x1 25.7 us: on_device(): lax.all_gather(inputs, 'col', axis=0, tiled=True)]
    convert_element_type x3 -> x2, other arithmetic: 9.8 us -> 3.24 us  [the longest x1 1.62 us: on_device(): in_grad = scatter(in_sum).astype(jnp.bfloat16)]
  transfers between devices with their start and end apart: 5 -> 2, of which waited for: 3 -> 2; matrix products, arithmetic and copies ran while one was open for 27% -> 12% of each run, Pallas kernels for 0% -> 0%
where the time goes in v1:
time: 207 us; the launch traced here: 206 us
  Pallas kernels  117 us (57%)
  waiting for transfers between devices  48.4 us (23%)
  matrix products  22.8 us (11%)
  between operations  14.1 us (7%)
  other arithmetic  3.24 us (2%)
    pallas_call x1, Pallas kernels, mix(): pl.pallas_call(functools.partial(mix_kernel, n, planes, units), out_shape...  117 us
    reduce_scatter x1, waiting for transfers between devices, on_device(): in_grad = scatter(in_sum).astype(jnp.bfloat16)  35.1 us
    dot_general x3, matrix products, contract_first(): lax.dot_general(left, right, (((0,), (0,)), ((), ())), preferred_element_...  22.8 us
    reduce_scatter x1, waiting for transfers between devices, on_device(): output = scatter(out_sum).astype(jnp.bfloat16)  12.6 us
  transfers between devices with their start and end apart: 2, of which 2 were waited for; matrix products, arithmetic and copies ran while one was open for 12% of the time, Pallas kernels for 0%

profile of v1, /device:TPU:0, one launch (start us, length us, event | category | flops | bytes accessed | tf_op | source)
XLA Modules:
  0.0 206.3 jit_solution(5963613822032308151)
XLA Ops:
  7.2 0.0 reduce-scatter.3.cloned.1.call-start
  7.2 116.7 %shard_map.92 = (bf16[256,2048]{1,0:T(8,128)(2,1)}, bf16[256,2048]{1,0:T(8,128)(2,1)}, bf16[256,3584]{1,0:T(8,128)(2,1)}, bf16[256,3584]{1,0:T(8,128)(2,1)}, bf1...) custom-call(bf16[32,2048]{1,0:T(8,128)(2,1)} %x_ref.1, bf16[32,2048]{1,0:T(8,128)(2,1)} %og_ref.1, ...), custom_call_target="tpu_custom_call" | custom-call | flops 22548578304 | bytes 88080384 | tf_op jit(solution)/shard_map/pallas_call | solution.py:376
  124.0 0.0 copy-start
  124.0 0.0 copy-start.3
  124.0 0.0 reduce-scatter.3.cloned.1.call-update
  124.0 0.0 reduce-scatter.5.cloned.1.call-start
  124.1 0.7 reduce-scatter.5.cloned.1.call-update
  124.8 0.4 copy-done
  125.2 0.6 copy-done.3
  125.8 0.0 copy-start.2
  125.8 7.6 %convolution_convert_fusion.2 = bf16[2048,3584]{1,0:T(8,128)(2,1)} fusion(bf16[256,2048]{1,0:T(8,128)(2,1)S(1)} %copy-done, bf16[256,3584]{1,0:T(8,128)(2,1)S(1)} %copy-done.3), kind=kOutput, calls=%fused_computation.2 | convolution fusion | flops 3765436416 | bytes 17563648 | tf_op jit(solution)/shard_map/dot_general | solution.py:17
  133.4 0.0 copy-done.2
  133.4 0.0 copy-start.1
  133.4 0.0 copy-start.4
  133.4 7.6 %convolution_convert_fusion.1 = bf16[2048,3584]{1,0:T(8,128)(2,1)} fusion(bf16[256,2048]{1,0:T(8,128)(2,1)S(1)} %copy-done, bf16[256,3584]{1,0:T(8,128)(2,1)S(1)} %copy-done.2), kind=kOutput, calls=%fused_computation.1 | convolution fusion | flops 3765436416 | bytes 17563648 | tf_op jit(solution)/shard_map/dot_general | solution.py:17
  141.0 0.0 copy-done.1
  141.0 0.0 copy-done.4
  141.0 7.6 %convolution_convert_fusion = bf16[3584,2048]{1,0:T(8,128)(2,1)} fusion(bf16[256,3584]{1,0:T(8,128)(2,1)S(1)} %copy-done.1, bf16[256,2048]{1,0:T(8,128)(2,1)S(1)} %copy-done.4), kind=kOutput, calls=%fused_computation | convolution fusion | flops 3765436416 | bytes 17563648 | tf_op jit(solution)/shard_map/dot_general | solution.py:17
  148.6 12.6 %reduce-scatter.3.cloned.1.call-done = f32[32,2048]{1,0:T(8,128)} async-done(((f32[256,2048]{1,0:T(8,128)}), f32[32,2048]{1,0:T(8,128)}) %reduce-scatter.3.cloned.1.call-update) | async-done | bytes 262160 | tf_op jit(solution)/shard_map/reduce_scatter | solution.py:434
  161.2 1.6 convert_element_type.15
  162.8 35.1 %reduce-scatter.5.cloned.1.call-done = f32[32,2048]{1,0:T(8,128)} async-done(((f32[256,2048]{1,0:T(8,128)}), f32[32,2048]{1,0:T(8,128)}) %reduce-scatter.5.cloned.1.call-update) | async-done | bytes 262160 | tf_op jit(solution)/shard_map/reduce_scatter | solution.py:435
  197.9 1.6 convert_element_type.16
Async XLA Ops:
  7.2 154.0 %reduce-scatter.3.cloned.1.call-start = ((), (), s32[]{:S(2)}) async-start(), calls=%async_computation.2 | async-start | bytes 2359296 | tf_op jit(solution)/shard_map/reduce_scatter | solution.py:434
  124.0 1.2 copy-start
  124.0 1.8 copy-start.3
  124.0 73.9 %reduce-scatter.5.cloned.1.call-start = ((), (), s32[]{:S(2)}) async-start(), calls=%async_computation.3 | async-start | bytes 2359296 | tf_op jit(solution)/shard_map/reduce_scatter | solution.py:435
  125.8 7.6 %copy-start.2 = (bf16[256,3584]{1,0:T(8,128)(2,1)S(1)}, bf16[256,3584]{1,0:T(8,128)(2,1)}, u32[]{:S(2)}) copy-start(bf16[256,3584]{1,0:T(8,128)(2,1)} %get-tuple-element.16) | copy-start | bytes 5505028
  133.4 7.6 %copy-start.1 = (bf16[256,3584]{1,0:T(8,128)(2,1)S(1)}, bf16[256,3584]{1,0:T(8,128)(2,1)}, u32[]{:S(2)}) copy-start(bf16[256,3584]{1,0:T(8,128)(2,1)} %get-tuple-element.17) | copy-start | bytes 5505028
  133.4 7.6 %copy-start.4 = (bf16[256,2048]{1,0:T(8,128)(2,1)S(1)}, bf16[256,2048]{1,0:T(8,128)(2,1)}, u32[]{:S(2)}) copy-start(bf16[256,2048]{1,0:T(8,128)(2,1)} %get-tuple-element.18) | copy-start | bytes 3145732
Sparse Core Ops, SparseCore 0:
  124.1 37.0 reduce-scatter.2
  163.5 34.3 reduce-scatter.4

commit v2 on v1

--- a/solution.py
+++ b/solution.py
@@ -35,12 +35,13 @@
 def mix_kernel(
     side, planes, units,
     x_ref, og_ref, wg_ref, wu_ref, wd_ref,
-    x_out, og_out, h_out, gp_out, up_out, acc_out, acc_in,
-    xf, of, wgu, wdn, p_gu, p_h, own_gu, own_h, r1_gu, r1_h, p2_gu, p2_h, r2_gu, r2_h,
-    full, stage, tmp,
+    x_out, og_out, h_out, gp_out, up_out, keep, *rest,
+):
+    parts = rest[: planes - 1]
+    (xf, of, wgu, wdn, p_gu, p_h, own_gu, own_h, r1_gu, r1_h, p2_gu, p2_h, r2_gu, r2_h,
+    full, stage, tmp, acc_out, acc_in, pair_send, pair_recv,
     gz_send, gz_recv, gs_send, gs_recv,
-    rs_send, rs_recv, ld_gu, ld_d, io_sem, st_sem,
-):
+    rs_send, rs_recv, ld_gu, ld_d, io_sem, st_sem, pr_send, pr_recv) = rest[planes - 1 :]
     n, unit = side, wgu.shape[-1]
     owners = n * n
     tokens, width = xf.shape
@@ -262,36 +263,45 @@
 
     tile = min(512, width)
 
-    def finish(par, i):
+    def finish(pair):
+        i = 2 * pair
         k = units + i
         s = k % RING
-        for d in range(1, n):
-            spread_second(par, i, d).wait_recv()
-        for a in range(3):
-            for owner in range(owners):
-                stage[a, pl.ds(owner * token_block, token_block), columns(i)] = full[
-                    i, slot_of(par, owner), a
-                ]
-        start(store(i))
-        wait(load_gu(k))
-        wait(load_d(k))
+        for par in range(2):
+            for d in range(1, n):
+                spread_second(par, i + par, d).wait_recv()
+            for a in range(3):
+                for owner in range(owners):
+                    stage[a, pl.ds(owner * token_block, token_block), columns(i + par)] = full[
+                        i + par, slot_of(par, owner), a
+                    ]
+            start(store(i + par))
+            wait(load_gu(k + par))
+            wait(load_d(k + par))
+        both = pl.ds(pl.multiple_of(i * unit, 128), 2 * unit)
 
         def add(t, carry):
             cols = pl.ds(pl.multiple_of(t * tile, 128), tile)
+            down = wdn[pl.ds(s, 2), :, cols].reshape(2 * unit, tile)
             acc_out[:, cols] += jnp.dot(
-                stage[0, :, columns(i)], wdn[s, :, cols], preferred_element_type=jnp.float32
+                stage[0, :, both], down, preferred_element_type=jnp.float32
             )
-            acc_in[:, cols] += contract_last(
-                stage[1, :, columns(i)], wgu[s, 0, cols, :]
-            ) + contract_last(stage[2, :, columns(i)], wgu[s, 1, cols, :])
+            total = acc_in[:, cols]
+            for par in range(2):
+                for a in range(2):
+                    total = total + contract_last(
+                        stage[1 + a, :, columns(i + par)], wgu[s + par, a, cols, :]
+                    )
+            acc_in[:, cols] = total
             return carry
 
         lax.fori_loop(0, width // tile, add, 0)
 
         @pl.when(k + RING < 2 * units)
         def _():
-            start(load_gu(k + RING))
-            start(load_d(k + RING))
+            for par in range(2):
+                start(load_gu(k + par + RING))
+                start(load_d(k + par + RING))
 
     pl.semaphore_wait(barrier, len(partners))
     gather_start(0, x_ref, xf)
@@ -306,9 +316,9 @@
     starts["grad"] = pairs
     starts["halfway1"] = pairs + LAG
     starts["gate"] = pairs + 2 * LAG
-    starts["forward"] = pairs + 3 * LAG
-    starts["finish"] = pairs + 4 * LAG
-    steps = pairs + 4 * LAG + pairs
+    starts["forward"] = starts["gate"] + 1
+    starts["finish"] = starts["gate"] + 2
+    steps = starts["finish"] + pairs
 
     def step(t, carry):
         def during(name, work):
@@ -329,10 +339,37 @@
         during("halfway1", functools.partial(halfway, 1))
         during("gate", gate)
         during("forward", forward)
-        during("finish", finish)
+
+        @pl.when(t >= starts["finish"])
+        def _():
+            finish(t - starts["finish"])
+
         return carry
 
     lax.fori_loop(0, steps, step, 0)
+
+    totals = (acc_out, acc_in)
+
+    def swap(a):
+        return pltpu.make_async_remote_copy(
+            src_ref=pair_send.at[a], dst_ref=pair_recv.at[a],
+            send_sem=pr_send.at[a], recv_sem=pr_recv.at[a],
+            device_id=sibling, device_id_type=MESH,
+        )
+
+    for a in range(2):
+        for p in range(planes):
+            pair_send[a, p] = totals[a][rows(2 * p + 1 - core), :].astype(jnp.bfloat16)
+        swap(a).start()
+    for a in range(2):
+        swap(a).wait_recv()
+        for d in range(planes):
+            p = plane(d)
+            value = totals[a][rows(2 * p + core), :] + pair_recv[a, p].astype(jnp.float32)
+            if d == 0:
+                keep[a] = value
+            else:
+                parts[d - 1][a] = value.astype(jnp.bfloat16)
 
     outs = [
         pltpu.make_async_copy(xf, x_out, io_sem.at[0]),
@@ -356,6 +393,8 @@
     gather_drain(0, x_ref, xf)
     gather_drain(1, og_ref, of)
     wait(outs)
+    for a in range(2):
+        swap(a).wait_send()
 
 
 def mix(mesh, inputs, gate_weight, up_weight, down_weight, out_grad):
@@ -368,6 +407,7 @@
     units = units_of(hidden)
     u = hidden // units
     tb = tokens // rows
+    share = tokens // cols
     bf, f32 = jnp.bfloat16, jnp.float32
     dma = pltpu.SemaphoreType.DMA
     vmem = pl.BlockSpec(memory_space=pltpu.VMEM)
@@ -381,11 +421,11 @@
             jax.ShapeDtypeStruct((tokens, hidden), bf),
             jax.ShapeDtypeStruct((tokens, hidden), bf),
             jax.ShapeDtypeStruct((tokens, hidden), bf),
-            jax.ShapeDtypeStruct((tokens, width), f32),
-            jax.ShapeDtypeStruct((tokens, width), f32),
-        ),
+            jax.ShapeDtypeStruct((2, share, width), f32),
+        )
+        + (jax.ShapeDtypeStruct((2, share, width), bf),) * (planes - 1),
         in_specs=[vmem, vmem, hbm, hbm, hbm],
-        out_specs=(hbm, hbm, hbm, hbm, hbm, vmem, vmem),
+        out_specs=(hbm, hbm, hbm, hbm, hbm, vmem) + (vmem,) * (planes - 1),
         scratch_shapes=[
             pltpu.VMEM((tokens, width), bf),
             pltpu.VMEM((tokens, width), bf),
@@ -404,6 +444,10 @@
             pltpu.VMEM((units, rows, 3, tb, u), bf),
             pltpu.VMEM((3, tokens, hidden), bf),
             pltpu.VMEM((2, rows, tb, u), f32),
+            pltpu.VMEM((tokens, width), f32),
+            pltpu.VMEM((tokens, width), f32),
+            pltpu.VMEM((2, planes, share, width), bf),
+            pltpu.VMEM((2, planes, share, width), bf),
             dma((2, planes - 1)),
             dma((2, planes - 1)),
             dma((2, planes)),
@@ -414,6 +458,8 @@
             dma((RING,)),
             dma((2,)),
             dma((3, units)),
+            dma((2,)),
+            dma((2,)),
         ],
         compiler_params=pltpu.CompilerParams(
             collective_id=0, has_side_effects=True, vmem_limit_bytes=60 * 2**20
@@ -424,18 +470,82 @@
     )(inputs, out_grad, gate_weight, up_weight, down_weight)
 
 
+def grads_kernel(first, x_ref, gp_ref, up_ref, h_ref, og_ref, gate_ref, up_out, down_ref):
+    step = pl.program_id(0)
+
+    def fill(left, right, out):
+        columns = out.shape[1]
+        tile = 512 if columns % 512 == 0 else 256
+        for t in range(columns // tile):
+            cols = slice(t * tile, (t + 1) * tile)
+            out[:, cols] = jnp.dot(
+                left, right[:, cols], preferred_element_type=jnp.float32
+            ).astype(out.dtype)
+
+    @pl.when(step < first)
+    def _():
+        left = x_ref[...].T
+        fill(left, gp_ref, gate_ref)
+        fill(left, up_ref, up_out)
+
+    @pl.when(step >= first)
+    def _():
+        fill(h_ref[...].T, og_ref, down_ref)
+
+
+def weight_grads(inputs, gate_part, up_part, hidden, out_grad):
+    tokens, width = inputs.shape
+    units = hidden.shape[1]
+    wide = 256
+    tall = 512 if units % 512 == 0 else 256
+    first, second = width // wide, units // tall
+    bf = jnp.bfloat16
+    whole = functools.partial(pl.BlockSpec, index_map=lambda i: (0, 0))
+    return pl.pallas_call(
+        functools.partial(grads_kernel, first),
+        grid=(first + second,),
+        out_shape=(
+            jax.ShapeDtypeStruct((width, units), bf),
+            jax.ShapeDtypeStruct((width, units), bf),
+            jax.ShapeDtypeStruct((units, width), bf),
+        ),
+        in_specs=[
+            pl.BlockSpec((tokens, wide), lambda i: (0, jnp.minimum(i, first - 1))),
+            whole((tokens, units)),
+            whole((tokens, units)),
+            pl.BlockSpec((tokens, tall), lambda i: (0, jnp.maximum(i - first, 0))),
+            whole((tokens, width)),
+        ],
+        out_specs=(
+            pl.BlockSpec((wide, units), lambda i: (jnp.minimum(i, first - 1), 0)),
+            pl.BlockSpec((wide, units), lambda i: (jnp.minimum(i, first - 1), 0)),
+            pl.BlockSpec((tall, width), lambda i: (jnp.maximum(i - first, 0), 0)),
+        ),
+        compiler_params=pltpu.CompilerParams(vmem_limit_bytes=40 * 2**20),
+        cost_estimate=pl.CostEstimate(
+            flops=6 * tokens * width * units,
+            bytes_accessed=6 * width * units,
+            transcendentals=0,
+        ),
+    )(inputs, gate_part, up_part, hidden, out_grad)
+
+
 def on_device(mesh, inputs, gate_weight, up_weight, down_weight, out_grad):
-    all_inputs, all_grads, hidden, gate_part, up_part, out_sum, in_sum = mix(
+    all_inputs, all_grads, hidden, gate_part, up_part, keep, *parts = mix(
         mesh, inputs, gate_weight, up_weight, down_weight, out_grad
     )
-    scatter = functools.partial(
-        lax.psum_scatter, axis_name="col", scatter_dimension=0, tiled=True
+    cols = mesh.shape["col"]
+    arrived = [
+        lax.ppermute(part, "col", [(c, (c + 2 * d + 2) % cols) for c in range(cols)])
+        for d, part in enumerate(parts)
+    ]
+    gate_grad, up_grad, down_grad = weight_grads(
+        all_inputs, gate_part, up_part, hidden, all_grads
     )
-    output = scatter(out_sum).astype(jnp.bfloat16)
-    in_grad = scatter(in_sum).astype(jnp.bfloat16)
-    gate_grad = contract_first(all_inputs, gate_part).astype(jnp.bfloat16)
-    up_grad = contract_first(all_inputs, up_part).astype(jnp.bfloat16)
-    down_grad = contract_first(hidden, all_grads).astype(jnp.bfloat16)
+    total = keep
+    for part in arrived:
+        total = total + part.astype(jnp.float32)
+    output, in_grad = total[0].astype(jnp.bfloat16), total[1].astype(jnp.bfloat16)
     return (output, in_grad, gate_grad, up_grad, down_grad)
 
 

time: 207 us -> 154 us (0.74)
  waiting for transfers between devices: 48.4 us -> 0.01 us
  Pallas kernels: 117 us -> 140 us
  matrix products: 22.8 us -> 0 us
  between operations: 14.1 us -> 0.67 us
  local copies, waits for them, and re-layouts: 1.05 us -> 7.67 us
  starting transfers between devices: 0.08 us -> 4.82 us
  other arithmetic: 3.24 us -> 0.12 us
    reduce_scatter x2 -> x0, waiting for transfers between devices: 47.7 us -> none  [the longest x1 35.1 us: on_device(): in_grad = scatter(in_sum).astype(jnp.bfloat16)]
    dot_general x3 -> x0, matrix products: 22.8 us -> none  [contract_first(): lax.dot_general(left, right, (((0,), (0,)), ((), ())), preferred_element_...]
    pallas_call x0 -> x1, Pallas kernels: none -> 21.3 us  [weight_grads(): pl.pallas_call(functools.partial(grads_kernel, first), grid=(first + seco...]
    unnamed x10 -> x12, local copies, waits for them, and re-layouts: 1.05 us -> 6.95 us
    ppermute x0 -> x3, starting transfers between devices: none -> 4.82 us  [on_device(): lax.ppermute(part, 'col', [(c, (c + 2 * d + 2) % cols) for c in range(col...]
    convert_element_type x2 -> x0, other arithmetic: 3.24 us -> none  [the longest x1 1.62 us: on_device(): in_grad = scatter(in_sum).astype(jnp.bfloat16)]
  transfers between devices with their start and end apart: 2 -> 3, of which waited for: 2 -> 0; matrix products, arithmetic and copies ran while one was open for 12% -> 0% of each run, Pallas kernels for 0% -> 14%
where the time goes in v2:
time: 154 us; the launch traced here: 153 us
  Pallas kernels  140 us (91%)
  local copies, waits for them, and re-layouts  7.67 us (5%)
  starting transfers between devices  4.82 us (3%)
    pallas_call x1, Pallas kernels, mix(): pl.pallas_call(functools.partial(mix_kernel, n, planes, units), out_shape...  119 us
    pallas_call x1, Pallas kernels, weight_grads(): pl.pallas_call(functools.partial(grads_kernel, first), grid=(first + seco...  21.3 us
    unnamed x12, local copies, waits for them, and re-layouts  6.95 us
    ppermute x3, starting transfers between devices, on_device(): lax.ppermute(part, 'col', [(c, (c + 2 * d + 2) % cols) for c in range(col...  4.82 us
  transfers between devices with their start and end apart: 3, of which 0 were waited for; matrix products, arithmetic and copies ran while one was open for 0% of the time, Pallas kernels for 14%

profile of v2, /device:TPU:0, one launch (start us, length us, event | category | flops | bytes accessed | tf_op | source)
XLA Modules:
  0.0 153.4 jit_solution(1245605681719677255)
XLA Ops:
  0.6 118.8 %shard_map.92 = (bf16[256,2048]{1,0:T(8,128)(2,1)}, bf16[256,2048]{1,0:T(8,128)(2,1)}, bf16[256,3584]{1,0:T(8,128)(2,1)}, bf16[256,3584]{1,0:T(8,128)(2,1)}, bf1...) custom-call(bf16[32,2048]{1,0:T(8,128)(2,1)} %x_ref.1, ...), custom_call_target="tpu_custom_call" | custom-call | flops 22548578304 | bytes 88080384 | tf_op jit(solution)/shard_map/pallas_call | solution.py:416
  119.4 2.4 %collective-permute-start = (bf16[2,32,2048]{2,1,0:T(8,128)(2,1)}, bf16[2,32,2048]{2,1,0:T(8,128)(2,1)S(1)}, u32[]{:S(2)}, u32[]{:S(2)}) collective-permute-start(bf16[2,32,2048]{2,1,0:T(8,128)(2,1)} %get-tuple-element.18), channel_id=1, source_target_pairs={{0,2},{1,3},{2,4},{3,5},{4,6},{5,7},{6,0},{7,1},{8,10},{9,11},{10,... | collective-permute-start | bytes 786440 | tf_op jit(solution)/shard_map/ppermute | solution.py:539
  121.8 2.3 %collective-permute-start.1 = (bf16[2,32,2048]{2,1,0:T(8,128)(2,1)}, bf16[2,32,2048]{2,1,0:T(8,128)(2,1)S(1)}, u32[]{:S(2)}, u32[]{:S(2)}) collective-permute-start(bf16[2,32,2048]{2,1,0:T(8,128)(2,1)} %get-tuple-element.19), channel_id=1, source_target_pairs={{0,4},{1,5},{2,6},{3,7},{4,0},{5,1},{6,2},{7,3},{8,12},{9,13},{10,... | collective-permute-start | bytes 786440 | tf_op jit(solution)/shard_map/ppermute | solution.py:539
  124.1 0.1 collective-permute-start.2
  124.3 0.0 copy-start
  124.3 1.5 copy-done
  125.8 0.0 copy-start.1
  125.8 1.5 copy-done.1
  127.3 0.0 copy-start.2
  127.3 1.5 copy-done.2
  128.8 0.0 copy-start.3
  128.8 1.2 copy-done.3
  130.0 0.0 copy-start.4
  130.0 1.2 copy-done.4
  131.2 0.0 copy-start.5
  131.2 21.3 %shard_map.93 = (bf16[2048,3584]{1,0:T(8,128)(2,1)}, bf16[2048,3584]{1,0:T(8,128)(2,1)}, bf16[3584,2048]{1,0:T(8,128)(2,1)}) custom-call(bf16[256,2048]{1,0:T(8,128)(2,1)S(1)} %copy-done.3, bf16[256,3584]{1,0:T(8,128)(2,1)S(1)} %copy-done.1, bf16[256,3584]{1,0:T(8,128)(2,1)S(1)} %copy-done.2, bf16[256,3584]{1,0:T(8,128)(2,1)S(1)} %copy-done, ...), custom_call_target="tpu_custom_call" | custom-call | flops 11274289152 | bytes 44040192 | tf_op jit(solution)/shard_map/pallas_call | solution.py:504
  152.5 0.0 collective-permute-done
  152.5 0.0 collective-permute-done.1
  152.5 0.0 collective-permute-done.2
  152.5 0.0 copy-done.5
  152.5 0.1 add_convert_fusion
  152.7 0.7 slice_bitcast_fusion
Async XLA Ops:
  119.4 33.1 %collective-permute-start = (bf16[2,32,2048]{2,1,0:T(8,128)(2,1)}, bf16[2,32,2048]{2,1,0:T(8,128)(2,1)S(1)}, u32[]{:S(2)}, u32[]{:S(2)}) collective-permute-start(bf16[2,32,2048]{2,1,0:T(8,128)(2,1)} %get-tuple-element.18), channel_id=1, source_target_pairs={{0,2},{1,3},{2,4},{3,5},{4,6},{5,7},{6,0},{7,1},{8,10},{9,11},{10,... | collective-permute-start | bytes 786440 | tf_op jit(solution)/shard_map/ppermute | solution.py:539
  121.8 30.7 %collective-permute-start.1 = (bf16[2,32,2048]{2,1,0:T(8,128)(2,1)}, bf16[2,32,2048]{2,1,0:T(8,128)(2,1)S(1)}, u32[]{:S(2)}, u32[]{:S(2)}) collective-permute-start(bf16[2,32,2048]{2,1,0:T(8,128)(2,1)} %get-tuple-element.19), channel_id=1, source_target_pairs={{0,4},{1,5},{2,6},{3,7},{4,0},{5,1},{6,2},{7,3},{8,12},{9,13},{10,... | collective-permute-start | bytes 786440 | tf_op jit(solution)/shard_map/ppermute | solution.py:539
  124.1 28.4 %collective-permute-start.2 = (bf16[2,32,2048]{2,1,0:T(8,128)(2,1)}, bf16[2,32,2048]{2,1,0:T(8,128)(2,1)S(1)}, u32[]{:S(2)}, u32[]{:S(2)}) collective-permute-start(bf16[2,32,2048]{2,1,0:T(8,128)(2,1)} %get-tuple-element.20), channel_id=1, source_target_pairs={{0,6},{1,7},{2,0},{3,1},{4,2},{5,3},{6,4},{7,5},{8,14},{9,15},{10,... | collective-permute-start | bytes 786440 | tf_op jit(solution)/shard_map/ppermute | solution.py:539
  124.3 1.5 copy-start
  125.8 1.5 copy-start.1
  127.3 1.5 copy-start.2
  128.8 1.2 copy-start.3
  130.0 1.2 copy-start.4
  131.2 21.3 %copy-start.5 = (f32[2,32,2048]{2,1,0:T(8,128)S(1)}, f32[2,32,2048]{2,1,0:T(8,128)}, u32[]{:S(2)}) copy-start(f32[2,32,2048]{2,1,0:T(8,128)} %get-tuple-element.17) | copy-start | bytes 1572868

commit v3 on v2

--- a/solution.py
+++ b/solution.py
@@ -35,13 +35,13 @@
 def mix_kernel(
     side, planes, units,
     x_ref, og_ref, wg_ref, wu_ref, wd_ref,
-    x_out, og_out, h_out, gp_out, up_out, keep, *rest,
+    xt_out, og_out, ht_out, gp_out, up_out, output, keep, *rest,
 ):
     parts = rest[: planes - 1]
     (xf, of, wgu, wdn, p_gu, p_h, own_gu, own_h, r1_gu, r1_h, p2_gu, p2_h, r2_gu, r2_h,
-    full, stage, tmp, acc_out, acc_in, pair_send, pair_recv,
+    full_h, full_g, xt, ht, hp, stage, tmp, acc_out, acc_in, pair_send, pair_recv, z_out, z_in,
     gz_send, gz_recv, gs_send, gs_recv,
-    rs_send, rs_recv, ld_gu, ld_d, io_sem, st_sem, pr_send, pr_recv) = rest[planes - 1 :]
+    rs_send, rs_recv, ld_gu, ld_d, io_sem, st_sem, pr_send, pr_recv, z_send, z_recv) = rest[planes - 1 :]
     n, unit = side, wgu.shape[-1]
     owners = n * n
     tokens, width = xf.shape
@@ -161,21 +161,25 @@
             device_id=line((mine + d) % n), device_id_type=MESH,
         )
 
-    def spread_first(par, i, d):
+    fulls = (full_h, full_g)
+
+    def spread_first(kind, par, i, d):
         mine_f, _, mine_s, line = firsts[par]
-        block = full.at[i, mine_f * n + mine_s]
+        block = fulls[kind].at[i, mine_f * n + mine_s]
         return pltpu.make_async_remote_copy(
             src_ref=block, dst_ref=block,
-            send_sem=rs_send.at[4, i, d - 1], recv_sem=rs_recv.at[4, i, d - 1],
+            send_sem=rs_send.at[4 + 2 * kind, i, d - 1],
+            recv_sem=rs_recv.at[4 + 2 * kind, i, d - 1],
             device_id=line((mine_s + d) % n), device_id_type=MESH,
         )
 
-    def spread_second(par, i, d):
+    def spread_second(kind, par, i, d):
         mine, line, _, _ = firsts[par]
-        blocks = full.at[i, pl.ds(mine * n, n)]
+        blocks = fulls[kind].at[i, pl.ds(mine * n, n)]
         return pltpu.make_async_remote_copy(
             src_ref=blocks, dst_ref=blocks,
-            send_sem=rs_send.at[5, i, d - 1], recv_sem=rs_recv.at[5, i, d - 1],
+            send_sem=rs_send.at[5 + 2 * kind, i, d - 1],
+            recv_sem=rs_recv.at[5 + 2 * kind, i, d - 1],
             device_id=line((mine + d) % n), device_id_type=MESH,
         )
 
@@ -198,14 +202,41 @@
         for d in range(1, n):
             first_send(0, par, i, d).start()
 
-    def project_grad(par, i):
+    tile = min(512, width)
+
+    def grad_pair(pair):
+        i = 2 * pair
         s = i % RING
-        wait(load_d(i))
-        value = contract_last(of[...], wdn[s])
-        put_partial(par, i, 0, value, p_h, own_h, 1)
-        start(load_d(i + RING))
-        for d in range(1, n):
-            first_send(1, par, i, d).start()
+        for par in range(2):
+            wait(load_d(i + par))
+            value = contract_last(of[...], wdn[s + par])
+            put_partial(par, i + par, 0, value, p_h, own_h, 1)
+            for d in range(1, n):
+                first_send(1, par, i + par, d).start()
+        for par in range(2):
+            for d in range(1, n):
+                spread_second(0, par, i + par, d).wait_recv()
+            for owner in range(owners):
+                hp[pl.ds(owner * token_block, token_block), par * unit:(par + 1) * unit] = (
+                    full_h[i + par, slot_of(par, owner), 0]
+                )
+        ht[pl.ds(pl.multiple_of(i * unit, 128), 2 * unit), :] = hp[...].T
+        store_h(i).start()
+
+        def add(t, carry):
+            cols = pl.ds(pl.multiple_of(t * tile, 128), tile)
+            down = wdn[pl.ds(s, 2), :, cols].reshape(2 * unit, tile)
+            acc_out[:, cols] += jnp.dot(
+                hp[...], down, preferred_element_type=jnp.float32
+            )
+            return carry
+
+        lax.fori_loop(0, width // tile, add, 0)
+
+        @pl.when(i + RING < units)
+        def _():
+            for par in range(2):
+                start(load_d(i + par + RING))
 
     def halfway(kind, par, i):
         mine = firsts[par][2]
@@ -231,37 +262,48 @@
             total = total + last[i, e, a].astype(jnp.float32)
         return total
 
-    def gate(par, i):
-        for kind in range(2):
-            for d in range(1, n):
-                second_send(kind, par, i, d).wait_recv()
+    def gate_hidden(par, i):
+        for d in range(1, n):
+            second_send(0, par, i, d).wait_recv()
+        gate_value = total_of(0, par, i, 0)
+        up_value = total_of(0, par, i, 1)
+        sig = jax.nn.sigmoid(gate_value)
+        mine = firsts[par][0] * n + firsts[par][2]
+        full_h[i, mine, 0] = (gate_value * sig * up_value).astype(jnp.bfloat16)
+        for d in range(1, n):
+            spread_first(0, par, i, d).start()
+
+    def gate_grads(par, i):
+        for d in range(1, n):
+            second_send(1, par, i, d).wait_recv()
         gate_value = total_of(0, par, i, 0)
         up_value = total_of(0, par, i, 1)
         hidden_grad = total_of(1, par, i, 0)
         sig = jax.nn.sigmoid(gate_value)
         mine = firsts[par][0] * n + firsts[par][2]
-        full[i, mine, 0] = (gate_value * sig * up_value).astype(jnp.bfloat16)
         slope = sig * (1.0 + gate_value * (1.0 - sig))
-        full[i, mine, 1] = (hidden_grad * up_value * slope).astype(jnp.bfloat16)
-        full[i, mine, 2] = (hidden_grad * gate_value * sig).astype(jnp.bfloat16)
-        for d in range(1, n):
-            spread_first(par, i, d).start()
-
-    def forward(par, i):
-        for d in range(1, n):
-            spread_first(par, i, d).wait_recv()
-        for d in range(1, n):
-            spread_second(par, i, d).start()
+        full_g[i, mine, 0] = (hidden_grad * up_value * slope).astype(jnp.bfloat16)
+        full_g[i, mine, 1] = (hidden_grad * gate_value * sig).astype(jnp.bfloat16)
+        for d in range(1, n):
+            spread_first(1, par, i, d).start()
+
+    def forward(kind, par, i):
+        for d in range(1, n):
+            spread_first(kind, par, i, d).wait_recv()
+        for d in range(1, n):
+            spread_second(kind, par, i, d).start()
+
+    def store_h(i):
+        strip = pl.ds(pl.multiple_of(i * unit, 128), 2 * unit)
+        return pltpu.make_async_copy(ht.at[strip], ht_out.at[strip], st_sem.at[2, i])
 
     def store(i):
         return [
             pltpu.make_async_copy(
                 stage.at[a, :, columns(i)], out.at[:, columns(i)], st_sem.at[a, i]
             )
-            for a, out in enumerate((h_out, gp_out, up_out))
+            for a, out in enumerate((gp_out, up_out))
         ]
-
-    tile = min(512, width)
 
     def finish(pair):
         i = 2 * pair
@@ -269,28 +311,22 @@
         s = k % RING
         for par in range(2):
             for d in range(1, n):
-                spread_second(par, i + par, d).wait_recv()
-            for a in range(3):
+                spread_second(1, par, i + par, d).wait_recv()
+            for a in range(2):
                 for owner in range(owners):
-                    stage[a, pl.ds(owner * token_block, token_block), columns(i + par)] = full[
+                    stage[a, pl.ds(owner * token_block, token_block), columns(i + par)] = full_g[
                         i + par, slot_of(par, owner), a
                     ]
             start(store(i + par))
             wait(load_gu(k + par))
-            wait(load_d(k + par))
-        both = pl.ds(pl.multiple_of(i * unit, 128), 2 * unit)
 
         def add(t, carry):
             cols = pl.ds(pl.multiple_of(t * tile, 128), tile)
-            down = wdn[pl.ds(s, 2), :, cols].reshape(2 * unit, tile)
-            acc_out[:, cols] += jnp.dot(
-                stage[0, :, both], down, preferred_element_type=jnp.float32
-            )
             total = acc_in[:, cols]
             for par in range(2):
                 for a in range(2):
                     total = total + contract_last(
-                        stage[1 + a, :, columns(i + par)], wgu[s + par, a, cols, :]
+                        stage[a, :, columns(i + par)], wgu[s + par, a, cols, :]
                     )
             acc_in[:, cols] = total
             return carry
@@ -301,7 +337,44 @@
         def _():
             for par in range(2):
                 start(load_gu(k + par + RING))
-                start(load_d(k + par + RING))
+
+    totals = (acc_out, acc_in)
+
+    def swap(a):
+        return pltpu.make_async_remote_copy(
+            src_ref=pair_send.at[a], dst_ref=pair_recv.at[a],
+            send_sem=pr_send.at[a], recv_sem=pr_recv.at[a],
+            device_id=sibling, device_id_type=MESH,
+        )
+
+    def swap_start(a):
+        for p in range(planes):
+            pair_send[a, p] = totals[a][rows(2 * p + 1 - core), :].astype(jnp.bfloat16)
+        swap(a).start()
+
+    def chip_sum(a, d):
+        p = plane(d)
+        return totals[a][rows(2 * p + core), :] + pair_recv[a, p].astype(jnp.float32)
+
+    def z_copy(d):
+        return pltpu.make_async_remote_copy(
+            src_ref=z_out.at[d - 1], dst_ref=z_in.at[d - 1],
+            send_sem=z_send.at[d - 1], recv_sem=z_recv.at[d - 1],
+            device_id=(row, plane(d) * 2 + core), device_id_type=MESH,
+        )
+
+    def z_start():
+        swap(0).wait_recv()
+        for d in range(1, planes):
+            z_out[d - 1] = chip_sum(0, d).astype(jnp.bfloat16)
+            z_copy(d).start()
+
+    def z_end():
+        total = chip_sum(0, 0)
+        for d in range(1, planes):
+            z_copy(d).wait_recv()
+            total = total + z_in[d - 1].astype(jnp.float32)
+        output[...] = total
 
     pl.semaphore_wait(barrier, len(partners))
     gather_start(0, x_ref, xf)
@@ -313,11 +386,13 @@
     starts = {}
     starts["project"] = 0
     starts["halfway0"] = LAG
+    starts["hidden"] = 2 * LAG
+    starts["spread0"] = 2 * LAG + 1
     starts["grad"] = pairs
     starts["halfway1"] = pairs + LAG
-    starts["gate"] = pairs + 2 * LAG
-    starts["forward"] = starts["gate"] + 1
-    starts["finish"] = starts["gate"] + 2
+    starts["grads"] = pairs + 2 * LAG
+    starts["spread1"] = starts["grads"] + 1
+    starts["finish"] = starts["grads"] + 2
     steps = starts["finish"] + pairs
 
     def step(t, carry):
@@ -332,13 +407,29 @@
         @pl.when(t == pairs)
         def _():
             gather_end(1, og_ref, of)
+            for c in range(0, width, 256):
+                xt[c:c + 256, :] = xf[:, c:c + 256].T
 
         during("project", project)
-        during("grad", project_grad)
         during("halfway0", functools.partial(halfway, 0))
+        during("hidden", gate_hidden)
+        during("spread0", functools.partial(forward, 0))
+
+        @pl.when(jnp.logical_and(t >= pairs, t < 2 * pairs))
+        def _():
+            grad_pair(t - pairs)
+
         during("halfway1", functools.partial(halfway, 1))
-        during("gate", gate)
-        during("forward", forward)
+        during("grads", gate_grads)
+        during("spread1", functools.partial(forward, 1))
+
+        @pl.when(t == 2 * pairs)
+        def _():
+            swap_start(0)
+
+        @pl.when(t == 2 * pairs + 1)
+        def _():
+            z_start()
 
         @pl.when(t >= starts["finish"])
         def _():
@@ -348,34 +439,17 @@
 
     lax.fori_loop(0, steps, step, 0)
 
-    totals = (acc_out, acc_in)
-
-    def swap(a):
-        return pltpu.make_async_remote_copy(
-            src_ref=pair_send.at[a], dst_ref=pair_recv.at[a],
-            send_sem=pr_send.at[a], recv_sem=pr_recv.at[a],
-            device_id=sibling, device_id_type=MESH,
-        )
-
-    for a in range(2):
-        for p in range(planes):
-            pair_send[a, p] = totals[a][rows(2 * p + 1 - core), :].astype(jnp.bfloat16)
-        swap(a).start()
-    for a in range(2):
-        swap(a).wait_recv()
-        for d in range(planes):
-            p = plane(d)
-            value = totals[a][rows(2 * p + core), :] + pair_recv[a, p].astype(jnp.float32)
-            if d == 0:
-                keep[a] = value
-            else:
-                parts[d - 1][a] = value.astype(jnp.bfloat16)
-
+    swap_start(1)
     outs = [
-        pltpu.make_async_copy(xf, x_out, io_sem.at[0]),
+        pltpu.make_async_copy(xt, xt_out, io_sem.at[0]),
         pltpu.make_async_copy(of, og_out, io_sem.at[1]),
     ]
     start(outs)
+    z_end()
+    swap(1).wait_recv()
+    keep[...] = chip_sum(1, 0)
+    for d in range(1, planes):
+        parts[d - 1][...] = chip_sum(1, d).astype(jnp.bfloat16)
 
     def drain(p, carry):
         for par in range(2):
@@ -384,9 +458,10 @@
                 for kind in range(2):
                     first_send(kind, par, i, d).wait_send()
                     second_send(kind, par, i, d).wait_send()
-                spread_first(par, i, d).wait_send()
-                spread_second(par, i, d).wait_send()
+                    spread_first(kind, par, i, d).wait_send()
+                    spread_second(kind, par, i, d).wait_send()
             wait(store(i))
+        store_h(2 * p).wait()
         return carry
 
     lax.fori_loop(0, pairs, drain, 0)
@@ -395,6 +470,8 @@
     wait(outs)
     for a in range(2):
         swap(a).wait_send()
+    for d in range(1, planes):
+        z_copy(d).wait_send()
 
 
 def mix(mesh, inputs, gate_weight, up_weight, down_weight, out_grad):
@@ -416,16 +493,17 @@
     return pl.pallas_call(
         functools.partial(mix_kernel, n, planes, units),
         out_shape=(
+            jax.ShapeDtypeStruct((width, tokens), bf),
             jax.ShapeDtypeStruct((tokens, width), bf),
-            jax.ShapeDtypeStruct((tokens, width), bf),
+            jax.ShapeDtypeStruct((hidden, tokens), bf),
             jax.ShapeDtypeStruct((tokens, hidden), bf),
             jax.ShapeDtypeStruct((tokens, hidden), bf),
-            jax.ShapeDtypeStruct((tokens, hidden), bf),
-            jax.ShapeDtypeStruct((2, share, width), f32),
-        )
-        + (jax.ShapeDtypeStruct((2, share, width), bf),) * (planes - 1),
+            jax.ShapeDtypeStruct((share, width), f32),
+            jax.ShapeDtypeStruct((share, width), f32),
+        )
+        + (jax.ShapeDtypeStruct((share, width), bf),) * (planes - 1),
         in_specs=[vmem, vmem, hbm, hbm, hbm],
-        out_specs=(hbm, hbm, hbm, hbm, hbm, vmem) + (vmem,) * (planes - 1),
+        out_specs=(hbm, hbm, hbm, hbm, hbm, vmem, vmem) + (vmem,) * (planes - 1),
         scratch_shapes=[
             pltpu.VMEM((tokens, width), bf),
             pltpu.VMEM((tokens, width), bf),
@@ -441,25 +519,33 @@
             pltpu.VMEM((units, n - 1, 1, tb, u), bf),
             pltpu.VMEM((units, n - 1, 2, tb, u), bf),
             pltpu.VMEM((units, n - 1, 1, tb, u), bf),
-            pltpu.VMEM((units, rows, 3, tb, u), bf),
-            pltpu.VMEM((3, tokens, hidden), bf),
+            pltpu.VMEM((units, rows, 1, tb, u), bf),
+            pltpu.VMEM((units, rows, 2, tb, u), bf),
+            pltpu.VMEM((width, tokens), bf),
+            pltpu.VMEM((hidden, tokens), bf),
+            pltpu.VMEM((tokens, 2 * u), bf),
+            pltpu.VMEM((2, tokens, hidden), bf),
             pltpu.VMEM((2, rows, tb, u), f32),
             pltpu.VMEM((tokens, width), f32),
             pltpu.VMEM((tokens, width), f32),
             pltpu.VMEM((2, planes, share, width), bf),
             pltpu.VMEM((2, planes, share, width), bf),
+            pltpu.VMEM((planes - 1, share, width), bf),
+            pltpu.VMEM((planes - 1, share, width), bf),
             dma((2, planes - 1)),
             dma((2, planes - 1)),
             dma((2, planes)),
             dma((2, planes)),
-            dma((6, units, n - 1)),
-            dma((6, units, n - 1)),
+            dma((8, units, n - 1)),
+            dma((8, units, n - 1)),
             dma((RING, 2)),
             dma((RING,)),
             dma((2,)),
             dma((3, units)),
             dma((2,)),
             dma((2,)),
+            dma((planes - 1,)),
+            dma((planes - 1,)),
         ],
         compiler_params=pltpu.CompilerParams(
             collective_id=0, has_side_effects=True, vmem_limit_bytes=60 * 2**20
@@ -470,37 +556,42 @@
     )(inputs, out_grad, gate_weight, up_weight, down_weight)
 
 
-def grads_kernel(first, x_ref, gp_ref, up_ref, h_ref, og_ref, gate_ref, up_out, down_ref):
+def grads_kernel(first, xt_ref, gp_ref, up_ref, ht_ref, og_ref, gate_ref, up_out, down_ref):
     step = pl.program_id(0)
 
     def fill(left, right, out):
-        columns = out.shape[1]
-        tile = 512 if columns % 512 == 0 else 256
-        for t in range(columns // tile):
-            cols = slice(t * tile, (t + 1) * tile)
-            out[:, cols] = jnp.dot(
-                left, right[:, cols], preferred_element_type=jnp.float32
+        rows = out.shape[0] // 4
+        for t in range(4):
+            part = slice(t * rows, (t + 1) * rows)
+            out[part, :] = jnp.dot(
+                left[part, :], right[...], preferred_element_type=jnp.float32
             ).astype(out.dtype)
 
     @pl.when(step < first)
     def _():
-        left = x_ref[...].T
-        fill(left, gp_ref, gate_ref)
-        fill(left, up_ref, up_out)
+        fill(xt_ref, gp_ref, gate_ref)
+        fill(xt_ref, up_ref, up_out)
 
     @pl.when(step >= first)
     def _():
-        fill(h_ref[...].T, og_ref, down_ref)
-
-
-def weight_grads(inputs, gate_part, up_part, hidden, out_grad):
-    tokens, width = inputs.shape
-    units = hidden.shape[1]
-    wide = 256
-    tall = 512 if units % 512 == 0 else 256
-    first, second = width // wide, units // tall
+        fill(ht_ref, og_ref, down_ref)
+
+
+def weight_grads(inputs_t, gate_part, up_part, hidden_t, out_grad):
+    width, tokens = inputs_t.shape
+    units = hidden_t.shape[0]
+    wide = 512 if units % 512 == 0 else 256
+    tall = 512 if width % 512 == 0 else 256
+    first, second = units // wide, width // tall
     bf = jnp.bfloat16
     whole = functools.partial(pl.BlockSpec, index_map=lambda i: (0, 0))
+
+    def early(i):
+        return (0, jnp.minimum(i, first - 1))
+
+    def late(i):
+        return (0, jnp.maximum(i - first, 0))
+
     return pl.pallas_call(
         functools.partial(grads_kernel, first),
         grid=(first + second,),
@@ -510,28 +601,28 @@
             jax.ShapeDtypeStruct((units, width), bf),
         ),
         in_specs=[
-            pl.BlockSpec((tokens, wide), lambda i: (0, jnp.minimum(i, first - 1))),
-            whole((tokens, units)),
-            whole((tokens, units)),
-            pl.BlockSpec((tokens, tall), lambda i: (0, jnp.maximum(i - first, 0))),
-            whole((tokens, width)),
+            whole((width, tokens)),
+            pl.BlockSpec((tokens, wide), early),
+            pl.BlockSpec((tokens, wide), early),
+            whole((units, tokens)),
+            pl.BlockSpec((tokens, tall), late),
         ],
         out_specs=(
-            pl.BlockSpec((wide, units), lambda i: (jnp.minimum(i, first - 1), 0)),
-            pl.BlockSpec((wide, units), lambda i: (jnp.minimum(i, first - 1), 0)),
-            pl.BlockSpec((tall, width), lambda i: (jnp.maximum(i - first, 0), 0)),
+            pl.BlockSpec((width, wide), early),
+            pl.BlockSpec((width, wide), early),
+            pl.BlockSpec((units, tall), late),
         ),
-        compiler_params=pltpu.CompilerParams(vmem_limit_bytes=40 * 2**20),
+        compiler_params=pltpu.CompilerParams(vmem_limit_bytes=60 * 2**20),
         cost_estimate=pl.CostEstimate(
             flops=6 * tokens * width * units,
             bytes_accessed=6 * width * units,
             transcendentals=0,
         ),
-    )(inputs, gate_part, up_part, hidden, out_grad)
+    )(inputs_t, gate_part, up_part, hidden_t, out_grad)
 
 
 def on_device(mesh, inputs, gate_weight, up_weight, down_weight, out_grad):
-    all_inputs, all_grads, hidden, gate_part, up_part, keep, *parts = mix(
+    inputs_t, all_grads, hidden_t, gate_part, up_part, output, keep, *parts = mix(
         mesh, inputs, gate_weight, up_weight, down_weight, out_grad
     )
     cols = mesh.shape["col"]
@@ -540,13 +631,12 @@
         for d, part in enumerate(parts)
     ]
     gate_grad, up_grad, down_grad = weight_grads(
-        all_inputs, gate_part, up_part, hidden, all_grads
+        inputs_t, gate_part, up_part, hidden_t, all_grads
     )
     total = keep
     for part in arrived:
         total = total + part.astype(jnp.float32)
-    output, in_grad = total[0].astype(jnp.bfloat16), total[1].astype(jnp.bfloat16)
-    return (output, in_grad, gate_grad, up_grad, down_grad)
+    return (output.astype(jnp.bfloat16), total.astype(jnp.bfloat16), gate_grad, up_grad, down_grad)
 
 
 def solution(mesh):

time: 154 us -> 147 us (0.955)
  local copies, waits for them, and re-layouts: 7.67 us -> 0.01 us
    unnamed x12 -> x4, local copies, waits for them, and re-layouts: 6.95 us -> 0.01 us
    pallas_call x1, Pallas kernels: 119 us -> 117 us  [mix(): pl.pallas_call(functools.partial(mix_kernel, n, planes, units), out_shape...]
  transfers between devices with their start and end apart: 3 -> 3, of which waited for: 0 -> 0; matrix products, arithmetic and copies ran while one was open for 0% -> 0% of each run, Pallas kernels for 14% -> 15%
where the time goes in v3:
time: 147 us
  Pallas kernels  139 us (95%)
  starting transfers between devices  5.87 us (4%)
    pallas_call x1, Pallas kernels, mix(): pl.pallas_call(functools.partial(mix_kernel, n, planes, units), out_shape...  117 us
    pallas_call x1, Pallas kernels, weight_grads(): pl.pallas_call(functools.partial(grads_kernel, first), grid=(first + seco...  21.7 us
    ppermute x3, starting transfers between devices, on_device(): lax.ppermute(part, 'col', [(c, (c + 2 * d + 2) % cols) for c in range(col...  5.87 us
  transfers between devices with their start and end apart: 3, of which 0 were waited for; matrix products, arithmetic and copies ran while one was open for 0% of the time, Pallas kernels for 15%

profile of v3, /device:TPU:0, one launch (start us, length us, event | category | flops | bytes accessed | tf_op | source)
XLA Modules:
  0.0 146.8 jit_solution(13224869836222998369)
XLA Ops:
  0.6 117.2 %shard_map.92 = (bf16[2048,256]{1,0:T(8,128)(2,1)}, bf16[256,2048]{1,0:T(8,128)(2,1)}, bf16[3584,256]{1,0:T(8,128)(2,1)}, bf16[256,3584]{1,0:T(8,128)(2,1)}, bf1...) custom-call(bf16[32,2048]{1,0:T(8,128)(2,1)} %x_ref.1, ...), custom_call_target="tpu_custom_call" | custom-call | flops 22548578304 | bytes 88080384 | tf_op jit(solution)/shard_map/pallas_call | solution.py:493
  117.9 3.4 %collective-permute-start = (bf16[32,2048]{1,0:T(8,128)(2,1)}, bf16[32,2048]{1,0:T(8,128)(2,1)S(1)}, u32[]{:S(2)}, u32[]{:S(2)}) collective-permute-start(bf16[32,2048]{1,0:T(8,128)(2,1)} %get-tuple-element.20), channel_id=1, source_target_pairs={{0,2},{1,3},{2,4},{3,5},{4,6},{5,7},{6,0},{7,1},{8,10},{9,11},{10,... | collective-permute-start | bytes 393224 | tf_op jit(solution)/shard_map/ppermute | solution.py:630
  121.3 1.2 collective-permute-start.1
  122.5 1.2 collective-permute-start.2
  123.7 0.0 copy-start.1
  123.7 0.0 copy-start
  123.7 21.7 %shard_map.93 = (bf16[2048,3584]{1,0:T(8,128)(2,1)}, bf16[2048,3584]{1,0:T(8,128)(2,1)}, bf16[3584,2048]{1,0:T(8,128)(2,1)}) custom-call(bf16[2048,256]{1,0:T(8,128)(2,1)} %get-tuple-element.23.xt_ref, bf16[256,3584]{1,0:T(8,128)(2,1)} %get-tuple-element.24.gp_ref, bf16[256,3584]{1,0:T(8,128)(2,1)} %get-tuple-element.25.up_ref, ...), custom_call_target="tpu_custom_call" | custom-call | flops 11274289152 | bytes 44040192 | tf_op jit(solution)/shard_map/pallas_call | solution.py:595
  145.4 0.0 copy-done.1
  145.4 0.7 convert_element_type.15
  146.1 0.0 collective-permute-done
  146.1 0.0 collective-permute-done.1
  146.1 0.0 collective-permute-done.2
  146.1 0.0 copy-done
  146.1 0.7 add_convert_fusion
Async XLA Ops:
  117.9 28.2 %collective-permute-start = (bf16[32,2048]{1,0:T(8,128)(2,1)}, bf16[32,2048]{1,0:T(8,128)(2,1)S(1)}, u32[]{:S(2)}, u32[]{:S(2)}) collective-permute-start(bf16[32,2048]{1,0:T(8,128)(2,1)} %get-tuple-element.20), channel_id=1, source_target_pairs={{0,2},{1,3},{2,4},{3,5},{4,6},{5,7},{6,0},{7,1},{8,10},{9,11},{10,... | collective-permute-start | bytes 393224 | tf_op jit(solution)/shard_map/ppermute | solution.py:630
  121.3 24.8 %collective-permute-start.1 = (bf16[32,2048]{1,0:T(8,128)(2,1)}, bf16[32,2048]{1,0:T(8,128)(2,1)S(1)}, u32[]{:S(2)}, u32[]{:S(2)}) collective-permute-start(bf16[32,2048]{1,0:T(8,128)(2,1)} %get-tuple-element.21), channel_id=1, source_target_pairs={{0,4},{1,5},{2,6},{3,7},{4,0},{5,1},{6,2},{7,3},{8,12},{9,13},{10,... | collective-permute-start | bytes 393224 | tf_op jit(solution)/shard_map/ppermute | solution.py:630
  122.5 23.6 %collective-permute-start.2 = (bf16[32,2048]{1,0:T(8,128)(2,1)}, bf16[32,2048]{1,0:T(8,128)(2,1)S(1)}, u32[]{:S(2)}, u32[]{:S(2)}) collective-permute-start(bf16[32,2048]{1,0:T(8,128)(2,1)} %get-tuple-element.22), channel_id=1, source_target_pairs={{0,6},{1,7},{2,0},{3,1},{4,2},{5,3},{6,4},{7,5},{8,14},{9,15},{10,... | collective-permute-start | bytes 393224 | tf_op jit(solution)/shard_map/ppermute | solution.py:630
  123.7 21.7 %copy-start.1 = (f32[32,2048]{1,0:T(8,128)S(1)}, f32[32,2048]{1,0:T(8,128)}, u32[]{:S(2)}) copy-start(f32[32,2048]{1,0:T(8,128)} %get-tuple-element.18) | copy-start | bytes 786436
  123.7 22.4 %copy-start = (f32[32,2048]{1,0:T(8,128)S(1)}, f32[32,2048]{1,0:T(8,128)}, u32[]{:S(2)}) copy-start(f32[32,2048]{1,0:T(8,128)} %get-tuple-element.19) | copy-start | bytes 786436

commit v4 on v3

--- a/solution.py
+++ b/solution.py
@@ -41,13 +41,16 @@
     (xf, of, wgu, wdn, p_gu, p_h, own_gu, own_h, r1_gu, r1_h, p2_gu, p2_h, r2_gu, r2_h,
     full_h, full_g, xt, ht, hp, stage, tmp, acc_out, acc_in, pair_send, pair_recv, z_out, z_in,
     gz_send, gz_recv, gs_send, gs_recv,
-    rs_send, rs_recv, ld_gu, ld_d, io_sem, st_sem, pr_send, pr_recv, z_send, z_recv) = rest[planes - 1 :]
+    rs_send, rs_recv, ld_gu, ld_d, io_sem, st_sem, pr_send, pr_recv, z_send, z_recv,
+     hf_send, hf_recv) = rest[planes - 1 :]
     n, unit = side, wgu.shape[-1]
     owners = n * n
     tokens, width = xf.shape
     token_block = tokens // owners
     share = tokens // (2 * planes)
     pairs = units // 2
+    piece, half_block = share // 2, token_block // 2
+    per_block = half_block // piece
     row, col = lax.axis_index("row"), lax.axis_index("col")
     my_y, my_x = row // n, row % n
     z, core = col // 2, col % 2
@@ -104,20 +107,24 @@
         start(load_gu(k))
         start(load_d(k))
 
-    def rows(c):
-        return pl.ds(pl.multiple_of(c * share, 16), share)
+    def rows(c, h):
+        at = (c // per_block) * token_block + h * half_block + (c % per_block) * piece
+        return pl.ds(pl.multiple_of(at, 16), piece)
 
     def gather_z(a, src, dst, d):
-        return pltpu.make_async_remote_copy(
-            src_ref=src, dst_ref=dst.at[rows(col)],
+        h = a % 2
+        return pltpu.make_async_remote_copy(
+            src_ref=src.at[pl.ds(h * piece, piece)], dst_ref=dst.at[rows(col, h)],
             send_sem=gz_send.at[a, d - 1], recv_sem=gz_recv.at[a, d - 1],
             device_id=(row, plane(d) * 2 + core), device_id_type=MESH,
         )
 
     def gather_s(a, src, dst, d):
+        h = a % 2
         c = ((z + planes - d) % planes) * 2 + core
         return pltpu.make_async_remote_copy(
-            src_ref=src if d == 0 else dst.at[rows(c)], dst_ref=dst.at[rows(c)],
+            src_ref=src.at[pl.ds(h * piece, piece)] if d == 0 else dst.at[rows(c, h)],
+            dst_ref=dst.at[rows(c, h)],
             send_sem=gs_send.at[a, d], recv_sem=gs_recv.at[a, d],
             device_id=sibling, device_id_type=MESH,
         )
@@ -126,7 +133,7 @@
         for d in range(1, planes):
             gather_z(a, src, dst, d).start()
         gather_s(a, src, dst, 0).start()
-        dst[rows(col), :] = src[...]
+        dst[rows(col, a % 2), :] = src[pl.ds((a % 2) * piece, piece), :]
 
     def gather_end(a, src, dst):
         for d in range(1, planes):
@@ -135,9 +142,11 @@
         for d in range(planes):
             gather_s(a, src, dst, d).wait_recv()
 
-    def gather_drain(a, src, dst):
+    def gather_left(a, src, dst):
         for d in range(1, planes):
             gather_z(a, src, dst, d).wait_send()
+
+    def gather_drain(a, src, dst):
         for d in range(planes):
             gather_s(a, src, dst, d).wait_send()
 
@@ -148,6 +157,17 @@
         return pltpu.make_async_remote_copy(
             src_ref=src.at[i, pl.ds(to * n, n)], dst_ref=dst.at[i, d - 1],
             send_sem=rs_send.at[2 * kind, i, d - 1], recv_sem=rs_recv.at[2 * kind, i, d - 1],
+            device_id=line(to), device_id_type=MESH,
+        )
+
+    def half_send(h, par, i, d):
+        mine, line, _, _ = firsts[par]
+        to = (mine + d) % n
+        part = pl.ds(h * half_block, half_block)
+        return pltpu.make_async_remote_copy(
+            src_ref=p_gu.at[i, pl.ds(to * n, n), :, part],
+            dst_ref=r1_gu.at[i, d - 1, :, :, part],
+            send_sem=hf_send.at[h, i, d - 1], recv_sem=hf_recv.at[h, i, d - 1],
             device_id=line(to), device_id_type=MESH,
         )
 
@@ -201,6 +221,24 @@
         start(load_gu(i + RING))
         for d in range(1, n):
             first_send(0, par, i, d).start()
+
+    def project_half(h, par, i):
+        mine = firsts[par][0]
+        part = pl.ds(h * half_block, half_block)
+        left = jnp.concatenate(
+            [xf[pl.ds(o * token_block + h * half_block, half_block), :] for o in range(owners)]
+        )
+        for a in range(2):
+            value = jnp.dot(left, wgu[i, a], preferred_element_type=jnp.float32)
+            for owner in range(owners):
+                block = value[owner * half_block:(owner + 1) * half_block]
+                slot = slot_of(par, owner)
+                tmp[a, slot, part] = block
+                p_gu[i, slot, a, part] = block.astype(jnp.bfloat16)
+            for s in range(n):
+                own_gu[i, s, a, part] = tmp[a, mine * n + s, part]
+        for d in range(1, n):
+            half_send(h, par, i, d).start()
 
     tile = min(512, width)
 
@@ -241,8 +279,20 @@
     def halfway(kind, par, i):
         mine = firsts[par][2]
         own, got, out = ((own_gu, r1_gu, p2_gu), (own_h, r1_h, p2_h))[kind]
-        for d in range(1, n):
-            first_send(kind, par, i, d).wait_recv()
+        if kind == 0:
+            @pl.when(i < RING)
+            def _():
+                for d in range(1, n):
+                    for h in range(2):
+                        half_send(h, par, i, d).wait_recv()
+
+            @pl.when(i >= RING)
+            def _():
+                for d in range(1, n):
+                    first_send(kind, par, i, d).wait_recv()
+        else:
+            for d in range(1, n):
+                first_send(kind, par, i, d).wait_recv()
         for d in range(1, n):
             s = (mine + d) % n
             for a in range(2 - kind):
@@ -349,12 +399,16 @@
 
     def swap_start(a):
         for p in range(planes):
-            pair_send[a, p] = totals[a][rows(2 * p + 1 - core), :].astype(jnp.bfloat16)
+            for h in range(2):
+                pair_send[a, p, pl.ds(h * piece, piece)] = totals[a][
+                    rows(2 * p + 1 - core, h), :
+                ].astype(jnp.bfloat16)
         swap(a).start()
 
     def chip_sum(a, d):
         p = plane(d)
-        return totals[a][rows(2 * p + core), :] + pair_recv[a, p].astype(jnp.float32)
+        mine = jnp.concatenate([totals[a][rows(2 * p + core, h), :] for h in range(2)])
+        return mine + pair_recv[a, p].astype(jnp.float32)
 
     def z_copy(d):
         return pltpu.make_async_remote_copy(
@@ -378,10 +432,28 @@
 
     pl.semaphore_wait(barrier, len(partners))
     gather_start(0, x_ref, xf)
+    gather_left(0, x_ref, xf)
+    gather_start(1, x_ref, xf)
     acc_out[...] = jnp.zeros_like(acc_out)
     acc_in[...] = jnp.zeros_like(acc_in)
-    gather_end(0, x_ref, xf)
-    gather_start(1, og_ref, of)
+    for h in range(2):
+        gather_end(h, x_ref, xf)
+        if h == 1:
+            gather_left(1, x_ref, xf)
+            gather_start(2, og_ref, of)
+            gather_start(3, og_ref, of)
+
+        def early(p, carry):
+            for par in range(2):
+                i = 2 * p + par
+                if h == 0:
+                    wait(load_gu(i))
+                project_half(h, par, i)
+                if h == 1:
+                    start(load_gu(i + RING))
+            return carry
+
+        lax.fori_loop(0, RING // 2, early, 0)
 
     starts = {}
     starts["project"] = 0
@@ -406,7 +478,8 @@
 
         @pl.when(t == pairs)
         def _():
-            gather_end(1, og_ref, of)
+            gather_end(2, og_ref, of)
+            gather_end(3, og_ref, of)
             for c in range(0, width, 256):
                 xt[c:c + 256, :] = xf[:, c:c + 256].T
 
@@ -437,7 +510,7 @@
 
         return carry
 
-    lax.fori_loop(0, steps, step, 0)
+    lax.fori_loop(RING // 2, steps, step, 0)
 
     swap_start(1)
     outs = [
@@ -455,8 +528,18 @@
         for par in range(2):
             i = 2 * p + par
             for d in range(1, n):
+                first_send(1, par, i, d).wait_send()
+
+                @pl.when(i < RING)
+                def _():
+                    for h in range(2):
+                        half_send(h, par, i, d).wait_send()
+
+                @pl.when(i >= RING)
+                def _():
+                    first_send(0, par, i, d).wait_send()
+
                 for kind in range(2):
-                    first_send(kind, par, i, d).wait_send()
                     second_send(kind, par, i, d).wait_send()
                     spread_first(kind, par, i, d).wait_send()
                     spread_second(kind, par, i, d).wait_send()
@@ -466,7 +549,10 @@
 
     lax.fori_loop(0, pairs, drain, 0)
     gather_drain(0, x_ref, xf)
-    gather_drain(1, og_ref, of)
+    gather_drain(1, x_ref, xf)
+    for a in (2, 3):
+        gather_left(a, og_ref, of)
+        gather_drain(a, og_ref, of)
     wait(outs)
     for a in range(2):
         swap(a).wait_send()
@@ -532,10 +618,10 @@
             pltpu.VMEM((2, planes, share, width), bf),
             pltpu.VMEM((planes - 1, share, width), bf),
             pltpu.VMEM((planes - 1, share, width), bf),
-            dma((2, planes - 1)),
-            dma((2, planes - 1)),
-            dma((2, planes)),
-            dma((2, planes)),
+            dma((4, planes - 1)),
+            dma((4, planes - 1)),
+            dma((4, planes)),
+            dma((4, planes)),
             dma((8, units, n - 1)),
             dma((8, units, n - 1)),
             dma((RING, 2)),
@@ -546,6 +632,8 @@
             dma((2,)),
             dma((planes - 1,)),
             dma((planes - 1,)),
+            dma((2, RING, n - 1)),
+            dma((2, RING, n - 1)),
         ],
         compiler_params=pltpu.CompilerParams(
             collective_id=0, has_side_effects=True, vmem_limit_bytes=60 * 2**20

time: 147 us -> 144 us (0.980)
  no operation moved by 1% of the time
where the time goes in v4:
time: 144 us
  Pallas kernels  138 us (96%)
  starting transfers between devices  4.42 us (3%)
    pallas_call x1, Pallas kernels, mix(): pl.pallas_call(functools.partial(mix_kernel, n, planes, units), out_shape...  116 us
    pallas_call x1, Pallas kernels, weight_grads(): pl.pallas_call(functools.partial(grads_kernel, first), grid=(first + seco...  21.7 us
    ppermute x3, starting transfers between devices, on_device(): lax.ppermute(part, 'col', [(c, (c + 2 * d + 2) % cols) for c in range(col...  4.42 us
  transfers between devices with their start and end apart: 3, of which 0 were waited for; matrix products, arithmetic and copies ran while one was open for 0% of the time, Pallas kernels for 15%

profile of v4, /device:TPU:0, one launch (start us, length us, event | category | flops | bytes accessed | tf_op | source)
XLA Modules:
  0.0 144.1 jit_solution(6018735266097282340)
XLA Ops:
  0.6 115.9 %shard_map.92 = (bf16[2048,256]{1,0:T(8,128)(2,1)}, bf16[256,2048]{1,0:T(8,128)(2,1)}, bf16[3584,256]{1,0:T(8,128)(2,1)}, bf16[256,3584]{1,0:T(8,128)(2,1)}, bf1...) custom-call(bf16[32,2048]{1,0:T(8,128)(2,1)} %x_ref.1, ...), custom_call_target="tpu_custom_call" | custom-call | flops 22548578304 | bytes 88080384 | tf_op jit(solution)/shard_map/pallas_call | solution.py:579
  116.5 2.0 %collective-permute-start = (bf16[32,2048]{1,0:T(8,128)(2,1)}, bf16[32,2048]{1,0:T(8,128)(2,1)S(1)}, u32[]{:S(2)}, u32[]{:S(2)}) collective-permute-start(bf16[32,2048]{1,0:T(8,128)(2,1)} %get-tuple-element.20), channel_id=1, source_target_pairs={{0,2},{1,3},{2,4},{3,5},{4,6},{5,7},{6,0},{7,1},{8,10},{9,11},{10,... | collective-permute-start | bytes 393224 | tf_op jit(solution)/shard_map/ppermute | solution.py:718
  118.5 2.3 %collective-permute-start.1 = (bf16[32,2048]{1,0:T(8,128)(2,1)}, bf16[32,2048]{1,0:T(8,128)(2,1)S(1)}, u32[]{:S(2)}, u32[]{:S(2)}) collective-permute-start(bf16[32,2048]{1,0:T(8,128)(2,1)} %get-tuple-element.21), channel_id=1, source_target_pairs={{0,4},{1,5},{2,6},{3,7},{4,0},{5,1},{6,2},{7,3},{8,12},{9,13},{10,... | collective-permute-start | bytes 393224 | tf_op jit(solution)/shard_map/ppermute | solution.py:718
  120.8 0.2 collective-permute-start.2
  121.0 0.0 copy-start.1
  121.0 0.0 copy-start
  121.0 21.7 %shard_map.93 = (bf16[2048,3584]{1,0:T(8,128)(2,1)}, bf16[2048,3584]{1,0:T(8,128)(2,1)}, bf16[3584,2048]{1,0:T(8,128)(2,1)}) custom-call(bf16[2048,256]{1,0:T(8,128)(2,1)} %get-tuple-element.23.xt_ref, bf16[256,3584]{1,0:T(8,128)(2,1)} %get-tuple-element.24.gp_ref, bf16[256,3584]{1,0:T(8,128)(2,1)} %get-tuple-element.25.up_ref, ...), custom_call_target="tpu_custom_call" | custom-call | flops 11274289152 | bytes 44040192 | tf_op jit(solution)/shard_map/pallas_call | solution.py:683
  142.7 0.0 copy-done.1
  142.7 0.7 convert_element_type.15
  143.3 0.0 collective-permute-done
  143.3 0.0 collective-permute-done.1
  143.3 0.0 collective-permute-done.2
  143.3 0.0 copy-done
  143.4 0.7 add_convert_fusion
Async XLA Ops:
  116.5 26.8 %collective-permute-start = (bf16[32,2048]{1,0:T(8,128)(2,1)}, bf16[32,2048]{1,0:T(8,128)(2,1)S(1)}, u32[]{:S(2)}, u32[]{:S(2)}) collective-permute-start(bf16[32,2048]{1,0:T(8,128)(2,1)} %get-tuple-element.20), channel_id=1, source_target_pairs={{0,2},{1,3},{2,4},{3,5},{4,6},{5,7},{6,0},{7,1},{8,10},{9,11},{10,... | collective-permute-start | bytes 393224 | tf_op jit(solution)/shard_map/ppermute | solution.py:718
  118.5 24.8 %collective-permute-start.1 = (bf16[32,2048]{1,0:T(8,128)(2,1)}, bf16[32,2048]{1,0:T(8,128)(2,1)S(1)}, u32[]{:S(2)}, u32[]{:S(2)}) collective-permute-start(bf16[32,2048]{1,0:T(8,128)(2,1)} %get-tuple-element.21), channel_id=1, source_target_pairs={{0,4},{1,5},{2,6},{3,7},{4,0},{5,1},{6,2},{7,3},{8,12},{9,13},{10,... | collective-permute-start | bytes 393224 | tf_op jit(solution)/shard_map/ppermute | solution.py:718
  120.8 22.5 %collective-permute-start.2 = (bf16[32,2048]{1,0:T(8,128)(2,1)}, bf16[32,2048]{1,0:T(8,128)(2,1)S(1)}, u32[]{:S(2)}, u32[]{:S(2)}) collective-permute-start(bf16[32,2048]{1,0:T(8,128)(2,1)} %get-tuple-element.22), channel_id=1, source_target_pairs={{0,6},{1,7},{2,0},{3,1},{4,2},{5,3},{6,4},{7,5},{8,14},{9,15},{10,... | collective-permute-start | bytes 393224 | tf_op jit(solution)/shard_map/ppermute | solution.py:718
  121.0 21.7 %copy-start.1 = (f32[32,2048]{1,0:T(8,128)S(1)}, f32[32,2048]{1,0:T(8,128)}, u32[]{:S(2)}) copy-start(f32[32,2048]{1,0:T(8,128)} %get-tuple-element.18) | copy-start | bytes 786436
  121.0 22.4 %copy-start = (f32[32,2048]{1,0:T(8,128)S(1)}, f32[32,2048]{1,0:T(8,128)}, u32[]{:S(2)}) copy-start(f32[32,2048]{1,0:T(8,128)} %get-tuple-element.19) | copy-start | bytes 786436

commit v5 on v4

--- a/solution.py
+++ b/solution.py
@@ -10,7 +10,6 @@
 
 MESH = pl.DeviceIdType.MESH
 RING = 4
-LAG = 2
 
 
 def contract_first(left, right):
@@ -457,14 +456,14 @@
 
     starts = {}
     starts["project"] = 0
-    starts["halfway0"] = LAG
-    starts["hidden"] = 2 * LAG
-    starts["spread0"] = 2 * LAG + 1
+    starts["halfway0"] = RING // 2
+    starts["hidden"] = starts["halfway0"] + 1
+    starts["spread0"] = starts["hidden"] + 1
     starts["grad"] = pairs
-    starts["halfway1"] = pairs + LAG
-    starts["grads"] = pairs + 2 * LAG
-    starts["spread1"] = starts["grads"] + 1
-    starts["finish"] = starts["grads"] + 2
+    starts["halfway1"] = pairs + 1
+    starts["grads"] = pairs + 2
+    starts["spread1"] = pairs + 3
+    starts["finish"] = pairs + 4
     steps = starts["finish"] + pairs
 
     def step(t, carry):

time: 144 us -> 144 us (level)
  no operation moved by 1% of the time
where the time goes in v5:
time: 144 us
  Pallas kernels  138 us (96%)
  starting transfers between devices  4.23 us (3%)
    pallas_call x1, Pallas kernels, mix(): pl.pallas_call(functools.partial(mix_kernel, n, planes, units), out_shape...  116 us
    pallas_call x1, Pallas kernels, weight_grads(): pl.pallas_call(functools.partial(grads_kernel, first), grid=(first + seco...  21.7 us
    ppermute x3, starting transfers between devices, on_device(): lax.ppermute(part, 'col', [(c, (c + 2 * d + 2) % cols) for c in range(col...  4.23 us
  transfers between devices with their start and end apart: 3, of which 0 were waited for; matrix products, arithmetic and copies ran while one was open for 0% of the time, Pallas kernels for 15%

profile of v5, /device:TPU:0, one launch (start us, length us, event | category | flops | bytes accessed | tf_op | source)
XLA Modules:
  0.0 143.9 jit_solution(2466966880389906249)
XLA Ops:
  0.6 116.0 %shard_map.92 = (bf16[2048,256]{1,0:T(8,128)(2,1)}, bf16[256,2048]{1,0:T(8,128)(2,1)}, bf16[3584,256]{1,0:T(8,128)(2,1)}, bf16[256,3584]{1,0:T(8,128)(2,1)}, bf1...) custom-call(bf16[32,2048]{1,0:T(8,128)(2,1)} %x_ref.1, ...), custom_call_target="tpu_custom_call" | custom-call | flops 22548578304 | bytes 88080384 | tf_op jit(solution)/shard_map/pallas_call | solution.py:578
  116.6 1.8 %collective-permute-start = (bf16[32,2048]{1,0:T(8,128)(2,1)}, bf16[32,2048]{1,0:T(8,128)(2,1)S(1)}, u32[]{:S(2)}, u32[]{:S(2)}) collective-permute-start(bf16[32,2048]{1,0:T(8,128)(2,1)} %get-tuple-element.20), channel_id=1, source_target_pairs={{0,2},{1,3},{2,4},{3,5},{4,6},{5,7},{6,0},{7,1},{8,10},{9,11},{10,... | collective-permute-start | bytes 393224 | tf_op jit(solution)/shard_map/ppermute | solution.py:717
  118.4 2.4 %collective-permute-start.1 = (bf16[32,2048]{1,0:T(8,128)(2,1)}, bf16[32,2048]{1,0:T(8,128)(2,1)S(1)}, u32[]{:S(2)}, u32[]{:S(2)}) collective-permute-start(bf16[32,2048]{1,0:T(8,128)(2,1)} %get-tuple-element.21), channel_id=1, source_target_pairs={{0,4},{1,5},{2,6},{3,7},{4,0},{5,1},{6,2},{7,3},{8,12},{9,13},{10,... | collective-permute-start | bytes 393224 | tf_op jit(solution)/shard_map/ppermute | solution.py:717
  120.7 0.1 collective-permute-start.2
  120.8 0.0 copy-start.1
  120.8 0.0 copy-start
  120.8 21.7 %shard_map.93 = (bf16[2048,3584]{1,0:T(8,128)(2,1)}, bf16[2048,3584]{1,0:T(8,128)(2,1)}, bf16[3584,2048]{1,0:T(8,128)(2,1)}) custom-call(bf16[2048,256]{1,0:T(8,128)(2,1)} %get-tuple-element.23.xt_ref, bf16[256,3584]{1,0:T(8,128)(2,1)} %get-tuple-element.24.gp_ref, bf16[256,3584]{1,0:T(8,128)(2,1)} %get-tuple-element.25.up_ref, ...), custom_call_target="tpu_custom_call" | custom-call | flops 11274289152 | bytes 44040192 | tf_op jit(solution)/shard_map/pallas_call | solution.py:682
  142.5 0.0 copy-done.1
  142.5 0.7 convert_element_type.15
  143.2 0.0 collective-permute-done
  143.2 0.0 collective-permute-done.1
  143.2 0.0 collective-permute-done.2
  143.2 0.0 copy-done
  143.2 0.7 add_convert_fusion
Async XLA Ops:
  116.6 26.6 %collective-permute-start = (bf16[32,2048]{1,0:T(8,128)(2,1)}, bf16[32,2048]{1,0:T(8,128)(2,1)S(1)}, u32[]{:S(2)}, u32[]{:S(2)}) collective-permute-start(bf16[32,2048]{1,0:T(8,128)(2,1)} %get-tuple-element.20), channel_id=1, source_target_pairs={{0,2},{1,3},{2,4},{3,5},{4,6},{5,7},{6,0},{7,1},{8,10},{9,11},{10,... | collective-permute-start | bytes 393224 | tf_op jit(solution)/shard_map/ppermute | solution.py:717
  118.4 24.8 %collective-permute-start.1 = (bf16[32,2048]{1,0:T(8,128)(2,1)}, bf16[32,2048]{1,0:T(8,128)(2,1)S(1)}, u32[]{:S(2)}, u32[]{:S(2)}) collective-permute-start(bf16[32,2048]{1,0:T(8,128)(2,1)} %get-tuple-element.21), channel_id=1, source_target_pairs={{0,4},{1,5},{2,6},{3,7},{4,0},{5,1},{6,2},{7,3},{8,12},{9,13},{10,... | collective-permute-start | bytes 393224 | tf_op jit(solution)/shard_map/ppermute | solution.py:717
  120.7 22.5 %collective-permute-start.2 = (bf16[32,2048]{1,0:T(8,128)(2,1)}, bf16[32,2048]{1,0:T(8,128)(2,1)S(1)}, u32[]{:S(2)}, u32[]{:S(2)}) collective-permute-start(bf16[32,2048]{1,0:T(8,128)(2,1)} %get-tuple-element.22), channel_id=1, source_target_pairs={{0,6},{1,7},{2,0},{3,1},{4,2},{5,3},{6,4},{7,5},{8,14},{9,15},{10,... | collective-permute-start | bytes 393224 | tf_op jit(solution)/shard_map/ppermute | solution.py:717
  120.8 21.7 %copy-start.1 = (f32[32,2048]{1,0:T(8,128)S(1)}, f32[32,2048]{1,0:T(8,128)}, u32[]{:S(2)}) copy-start(f32[32,2048]{1,0:T(8,128)} %get-tuple-element.18) | copy-start | bytes 786436
  120.8 22.4 %copy-start = (f32[32,2048]{1,0:T(8,128)S(1)}, f32[32,2048]{1,0:T(8,128)}, u32[]{:S(2)}) copy-start(f32[32,2048]{1,0:T(8,128)} %get-tuple-element.19) | copy-start | bytes 786436
